TPU v7x, 128 devices: a whole 4x4x4 slice. The times are simulated.
128 devices in a mesh: band: 4 (over y), base: 32 (over z, x, core).
Axes of the slice: x: 4, y: 4, z: 4, core: 2. Of those that a mesh axis runs over, the one named last changes fastest.
Arguments:
- visibilities: bfloat16 [8, 64, 256, 256], P(None, 'base', 'band'), may hold values from -6 to 6
- model: bfloat16 [8, 64, 256, 256], P(None, 'base', 'band'), may hold values from -6 to 6
- start_gains: float32 [8, 128, 512], P(None, 'band', 'base'), may hold values from -1.5 to 2.5
- penalty: float32 [512], P('base'), may hold values from 0.5 to 5
- pairs: int32 [64, 2], P('base'), may hold values from 0 to 31, as said below
- flags: int32 [64, 256], P('base'), may hold values 0 or 1
- chan_band: int32 [256], P('band'), may hold values from 0 to 127, as said below
Outputs:
- gains: float32 [8, 128, 512], P(None, 'band', 'base')
- coefficients: float32 [8, 9, 512], P(None, None, 'base')
Inputs may be any that keep to these rules, and one draw needn't show every extreme that they name: `pairs`: each tile joins blocks a <= b, and no two tiles join the same pair of blocks. `chan_band`: the 64 channels of the k-th block of 64 channels map, never falling, onto the intervals k * 32 to k * 32 + 31, each interval holding one channel or more.
All inputs are finite; a program needn't handle non-finite values. No bound on the sum of `flags` on one device may be relied on, other than what follows from the above.
Results may differ from a plain program's by a relative error of at most 0.0003.
Values sent between devices are 32-bit elements; how exact they have to be, the bound alone decides.
A program may use at most 128 MiB of HBM per device.

v0:
```python
import functools

import jax
import jax.numpy as jnp
from jax import lax
from jax.experimental import pallas as pl
from jax.experimental.pallas import tpu as pltpu
from jax.sharding import PartitionSpec as P

BLOCK = 16
NPOLY = 9
ITERS = 3
RIDGE = 0.5
MESH = pl.DeviceIdType.MESH
F32 = jnp.float32
BF16 = jnp.bfloat16
SIDE = 4
CHIPS = SIDE * SIDE
BANDS = 4
TILES = 2
CHANS = 64
CELLS = BLOCK * BLOCK
SOLS = 32
LANES = 128
ROWS = SOLS + SOLS // 2
NCOEF = 48
PAIRS = [(0, 1), (0, 2), (0, 3), (1, 2), (1, 3), (2, 3)]


def lanes(x, idx):
    numbers = lax.GatherDimensionNumbers(
        offset_dims=(),
        collapsed_slice_dims=(1,),
        start_index_map=(1,),
        operand_batching_dims=(0,),
        start_indices_batching_dims=(0,),
    )
    return lax.gather(
        x, idx[..., None], numbers, (1, 1), mode=lax.GatherScatterMode.PROMISE_IN_BOUNDS
    )


def iota(shape, axis):
    return lax.broadcasted_iota(jnp.int32, shape, axis)


def merge(a, b, lane, bit):
    clear = (lane & bit) == 0
    return jnp.where(clear, a, b) + lanes(jnp.where(clear, b, a), lane ^ bit)


def merge_all(arrays, lane, top):
    bit = top
    while len(arrays) > 1:
        half = len(arrays) // 2
        arrays = [merge(a, b, lane, bit) for a, b in zip(arrays[:half], arrays[half:])]
        bit //= 2
    return arrays[0]


def mul(a, b):
    return (a[0] * b[0] - a[1] * b[1], a[0] * b[1] + a[1] * b[0])


def mul_conj(a, b):
    return (a[0] * b[0] + a[1] * b[1], a[0] * b[1] - a[1] * b[0])


def conj(a):
    return (a[0], -a[1])


def add(*terms):
    re, im = terms[0]
    for t in terms[1:]:
        re, im = re + t[0], im + t[1]
    return (re, im)


def scaled(a, r):
    return (a[0] * r, a[1] * r)


def outer(j):
    c = [(j[k], j[4 + k]) for k in range(4)]
    q00 = c[0][0] * c[0][0] + c[0][1] * c[0][1] + c[2][0] * c[2][0] + c[2][1] * c[2][1]
    q11 = c[1][0] * c[1][0] + c[1][1] * c[1][1] + c[3][0] * c[3][0] + c[3][1] * c[3][1]
    q01 = add(mul_conj(c[0], c[1]), mul_conj(c[2], c[3]))
    return q00, q11, q01


def station_terms(load, jp, jq):
    p = [(jp[k], jp[4 + k]) for k in range(4)]
    q = [(jq[k], jq[4 + k]) for k in range(4)]
    cross = {}
    for ab in range(4):
        for cd in range(4):
            cross[ab, cd] = (load(4 * ab + cd), load(16 + 4 * ab + cd))
    gp, gq = [], []
    for a in range(2):
        for d in range(2):
            gp.append(
                add(
                    *[
                        mul(cross[2 * a + b, 2 * d + c], q[2 * b + c])
                        for b in range(2)
                        for c in range(2)
                    ]
                )
            )
            gq.append(
                add(
                    *[
                        mul_conj(cross[2 * b + a, 2 * c + d], p[2 * b + c])
                        for b in range(2)
                        for c in range(2)
                    ]
                )
            )
    diag = [load(32 + k) for k in range(4)]
    off = {pair: (load(36 + 2 * n), load(37 + 2 * n)) for n, pair in enumerate(PAIRS)}
    q00, q11, q01 = outer(jq)
    two = scaled(q01, 2.0)
    hp = [
        diag[0] * q00 + diag[1] * q11 + mul_conj(conj(off[0, 1]), two)[0],
        diag[2] * q00 + diag[3] * q11 + mul_conj(conj(off[2, 3]), two)[0],
        *add(
            scaled(off[0, 2], q00),
            mul(off[0, 3], q01),
            mul_conj(q01, off[1, 2]),
            scaled(off[1, 3], q11),
        ),
    ]
    r00, r11, r01 = outer(jp)
    two = scaled(r01, 2.0)
    hq = [
        diag[0] * r00 + diag[2] * r11 + mul_conj(off[0, 2], two)[0],
        diag[1] * r00 + diag[3] * r11 + mul_conj(off[1, 3], two)[0],
        *add(
            scaled(conj(off[0, 1]), r00),
            mul_conj(off[0, 3], r01),
            mul_conj(r01, off[1, 2]),
            scaled(conj(off[2, 3]), r11),
        ),
    ]
    gp = [g[0] for g in gp] + [g[1] for g in gp]
    gq = [g[0] for g in gq] + [g[1] for g in gq]
    return gp, hp, gq, hq


def kernel(
    vis_hbm, mdl_hbm, start_hbm, pen_hbm, pairs_hbm, flags_hbm, chan_hbm,
    gains_out, coeff_out,
    vis, mdl, start, pen_in, pairs, flags, chan,
    vf, mf, coef, every, terms, sterms, sbuf, rbuf, prec, pv, spv, wrec, wsum, swsum,
    basis, scale, pen, cons, dual, ginv,
    loc, ag_s, ag_r, sx_s, sx_r, ts_s, ts_r, rs_s, rs_r, ps_s, ps_r, one,
):
    band = lax.axis_index("band")
    base = lax.axis_index("base")
    core = base % 2
    chip = base // 2
    cz = chip // SIDE
    cx = chip % SIDE
    sibling = chip * 2 + (1 - core)

    def peer_chip(r):
        return ((cz + r // SIDE) % SIDE) * SIDE + (cx + r % SIDE) % SIDE

    def copy(src, dst, send, recv, band_to, base_to):
        return pltpu.make_async_remote_copy(
            src_ref=src, dst_ref=dst, send_sem=send, recv_sem=recv,
            device_id=(band_to, base_to), device_id_type=MESH,
        )

    def to_chips(make):
        def step(r, carry):
            k = peer_chip(CHIPS - r)
            make(k).start()
            return carry

        lax.fori_loop(1, CHIPS, step, 0)

    local = [
        pltpu.make_async_copy(src, dst, loc.at[n])
        for n, (src, dst) in enumerate(
            [
                (start_hbm, start), (pairs_hbm, pairs), (flags_hbm, flags), (chan_hbm, chan),
                (pen_hbm, pen_in), (mdl_hbm, mdl), (vis_hbm, vis),
            ]
        )
    ]
    for c in local:
        c.start()

    barrier = pltpu.get_barrier_semaphore()

    def greet_chip(r, carry):
        pl.semaphore_signal(
            barrier, inc=1, device_id=(band, peer_chip(r) * 2 + core), device_id_type=MESH
        )
        return carry

    lax.fori_loop(1, CHIPS, greet_chip, 0)
    pl.semaphore_signal(barrier, inc=1, device_id=(band, sibling), device_id_type=MESH)

    def greet_band(r, carry):
        pl.semaphore_signal(
            barrier, inc=1, device_id=((band + r) % BANDS, base), device_id_type=MESH
        )
        return carry

    lax.fori_loop(1, BANDS, greet_band, 0)

    lane8 = iota((8, LANES), 1)
    row8 = iota((8, LANES), 0)
    for c in local[:5]:
        c.wait()
    mine = jnp.concatenate([start[k] for k in range(8)], axis=1)
    every[0, core, chip] = mine
    cons[...] = mine
    dual[...] = jnp.zeros_like(mine)

    pl.semaphore_wait(barrier, CHIPS + BANDS - 1)

    def send_gains(it):
        to_chips(
            lambda k: copy(
                every.at[it, core, chip], every.at[it, core, chip], ag_s.at[it], ag_r.at[it],
                band, 2 * k + core,
            )
        )

    send_gains(0)

    ends = [pairs[t, side] for t in range(TILES) for side in range(2)]
    named = jnp.zeros((8, LANES), jnp.int32)
    for e, b in enumerate(ends):
        named = jnp.where(row8 == e, b, named)
    pv[...] = named
    pairs_copy = copy(pv, spv, one.at[0], one.at[1], band, sibling)
    pairs_copy.start()

    cell = iota((1, CELLS), 1)
    eye = (cell // BLOCK == cell % BLOCK).astype(F32)
    weights = []
    for t in range(TILES):
        same = jnp.where(ends[2 * t] == ends[2 * t + 1], 1.0, 0.0)
        weights.append(flags[t : t + 1, :].astype(F32) * (1.0 - same * eye))
    both = jnp.concatenate([*weights, jnp.zeros((6, CELLS), F32)], axis=0).astype(BF16)
    fold_row = iota((CELLS, LANES), 0)
    fold_lane = iota((CELLS, LANES), 1) % BLOCK
    at_first = jnp.dot(
        both, (fold_row // BLOCK == fold_lane).astype(F32).astype(BF16),
        preferred_element_type=F32,
    )
    at_second = jnp.dot(
        both, (fold_row % BLOCK == fold_lane).astype(F32).astype(BF16),
        preferred_element_type=F32,
    )
    partial = jnp.zeros((8, LANES), F32)
    for e, b in enumerate(ends):
        t = e // 2
        at_end = (at_second if e % 2 else at_first)[t : t + 1, :]
        here = (row8 == (b >> 3)) & (lane8 // BLOCK == (b & 7))
        partial = partial + jnp.where(here, jnp.broadcast_to(at_end, (8, LANES)), 0.0)
    wrec[chip] = partial
    to_chips(
        lambda k: copy(wrec.at[chip], wrec.at[chip], one.at[2], one.at[3], band, 2 * k + core)
    )

    sol = band * SOLS + iota((SOLS, CHANS), 0)
    chan_row = chan[...]
    member = (jnp.broadcast_to(chan_row, (SOLS, CHANS)) == sol).astype(F32)
    where_c = (band * CHANS + iota((SOLS, CHANS), 1)).astype(F32)
    xpos = -1.0 + (2.0 * where_c + 1.0) / (CHANS * BANDS)
    chans = jnp.sum(member, axis=1, keepdims=True)
    centre = jnp.broadcast_to(
        jnp.sum(member * xpos, axis=1, keepdims=True) / chans, (SOLS, LANES)
    )
    cheb = [jnp.ones_like(centre), centre]
    for _ in range(2, NPOLY):
        cheb.append(2.0 * centre * cheb[-1] - cheb[-2])
    for k in range(NPOLY):
        basis[k] = cheb[k]
    member2 = jnp.concatenate([member, member], axis=1).astype(BF16)

    for c in local[5:]:
        c.wait()

    def collapse(t, carry):
        w = jnp.where(t == 0, weights[0], weights[1])
        for k in range(8):
            vf[k] = vis[k, t].astype(F32)
            mf[k] = mdl[k, t].astype(F32) * w

        def put(n, product):
            high = product.astype(BF16)
            low = (product - high.astype(F32)).astype(BF16)
            coef[n, t] = jnp.dot(
                member2, jnp.concatenate([high, low], axis=0), preferred_element_type=F32
            )

        for ab in range(4):
            vr, vi = vf[ab], vf[4 + ab]
            for cd in range(4):
                mr, mi = mf[cd], mf[4 + cd]
                put(4 * ab + cd, vr * mr + vi * mi)
                put(16 + 4 * ab + cd, vi * mr - vr * mi)
        for ab in range(4):
            put(32 + ab, mf[ab] * mf[ab] + mf[4 + ab] * mf[4 + ab])
        for n, (x, y) in enumerate(PAIRS):
            put(36 + 2 * n, mf[x] * mf[y] + mf[4 + x] * mf[4 + y])
            put(37 + 2 * n, mf[4 + x] * mf[y] - mf[x] * mf[4 + y])
        return carry

    lax.fori_loop(0, TILES, collapse, 0)

    def all_of(buffer, sem):
        part = buffer.at[pl.ds(0, CHIPS - 1)]
        pltpu.make_async_copy(part, part, sem).wait()

    all_of(wrec, one.at[3])
    wsum[...] = functools.reduce(lambda a, b: a + b, [wrec[k] for k in range(CHIPS)])
    sums_copy = copy(wsum, swsum, one.at[4], one.at[5], band, sibling)
    sums_copy.start()
    pairs_copy.wait_recv()
    sums_copy.wait_recv()
    row = wsum[pl.ds(base // 8, 1), :] + swsum[pl.ds(base // 8, 1), :]
    row = jnp.broadcast_to(row, (8, LANES))
    row = lanes(row, (base % 8) * BLOCK + lane8 % BLOCK)
    counts = chans * jnp.broadcast_to(row[0:1, :], (SOLS, LANES))
    scale[...] = 1.0 / jnp.maximum(counts, 1.0)
    pen[...] = jnp.broadcast_to(
        jnp.concatenate([pen_in[...]] * 8, axis=1), (8, LANES)
    )

    def total_of(it, values):
        lane = iota((SOLS, LANES), 1)
        columns = jnp.zeros((SOLS, LANES), F32)
        for k in range(NPOLY):
            columns = jnp.where(lane == k, basis[k], columns)
        rows = [jnp.sum(basis[k] * values, axis=0, keepdims=True) for k in range(NPOLY)]
        gram = [jnp.sum(basis[k] * columns, axis=0, keepdims=True) for k in range(NPOLY)]
        pad = [jnp.zeros((16 - NPOLY, LANES), F32)]
        prec[it, band] = jnp.concatenate(rows + pad + gram + pad, axis=0)

        def step(r, carry):
            copy(
                prec.at[it, band], prec.at[it, band], ps_s.at[it], ps_r.at[it],
                (band + r) % BANDS, base,
            ).start()
            return carry

        lax.fori_loop(1, BANDS, step, 0)

    def coefficients(it, first):
        part = prec.at[it, pl.ds(0, BANDS - 1)]
        pltpu.make_async_copy(part, part, ps_r.at[it]).wait()
        total = prec[it, 0] + prec[it, 1] + prec[it, 2] + prec[it, 3]

        def invert():
            r, l = iota((16, LANES), 0), iota((16, LANES), 1)
            m = total[16:, :] + jnp.where((r == l) & (r < NPOLY), RIDGE, 0.0)
            m = m + jnp.where((l == r + 16) & (r < NPOLY), 1.0, 0.0)
            for p in range(NPOLY):
                pivot = m[p : p + 1, :] / m[p : p + 1, p : p + 1]
                m = jnp.where(r == p, pivot, m - m[:, p : p + 1] * pivot)
            for k in range(NPOLY):
                ginv[k] = jnp.broadcast_to(m[:, 16 + k : 17 + k], (16, LANES))

        if first is not None:
            pl.when(first)(invert)
        out = ginv[0] * total[0:1, :]
        for k in range(1, NPOLY):
            out = out + ginv[k] * total[k : k + 1, :]
        return out

    step_rows = 16
    lane = iota((step_rows, LANES), 1)
    inner = lane % BLOCK
    natural = (inner % 8) * BLOCK + (inner // 8) * 8 + lane // BLOCK

    def iteration(it, carry):
        @pl.when(it > 0)
        def _():
            every[it, core, chip] = every[ITERS, core, chip]
            send_gains(it)
            coeff = coefficients(it - 1, it == 1)
            agreed = basis[0] * coeff[0:1, :]
            for k in range(1, NPOLY):
                agreed = agreed + basis[k] * coeff[k : k + 1, :]
            dual[...] = dual[...] + every[it, core, chip] - agreed
            cons[...] = agreed

        all_of(every.at[it, core], ag_r.at[it])
        across = copy(
            every.at[it, core], every.at[it, core], sx_s.at[it], sx_r.at[it], band, sibling
        )
        across.start()
        incoming = every.at[it, 1 - core]
        pltpu.make_async_copy(incoming, incoming, sx_r.at[it]).wait()

        def tile(t, carry):
            first, second = pairs[t, 0], pairs[t, 1]
            packed = []
            for part in range(2):
                rows = pl.ds(part * step_rows, step_rows)
                of_p = every[it, first & 1, first >> 1, rows, :]
                of_q = every[it, second & 1, second >> 1, rows, :]
                jq = [lanes(of_q, k * BLOCK + inner) for k in range(8)]
                gp, hp, gq, hq = [], [], [], []
                for half in range(2):
                    jp = [lanes(of_p, k * BLOCK + half * 8 + lane // BLOCK) for k in range(8)]

                    def load(n):
                        return coef[n, t, rows, pl.ds(half * LANES, LANES)]

                    a, b, c, d = station_terms(load, jp, jq)
                    gp.append(a)
                    hp.append(b)
                    gq.append(c)
                    hq.append(d)
                terms[it, 2 * t, rows, :] = lanes(merge_all(gp[0] + gp[1], lane, 8), natural)
                summed = [x + y for x, y in zip(gq[0], gq[1])]
                terms[it, 2 * t + 1, rows, :] = merge_all(summed, lane, 64)
                packed.append((hp, [x + y for x, y in zip(hq[0], hq[1])]))
            rows = pl.ds(SOLS, step_rows)
            (hp0, hq0), (hp1, hq1) = packed
            arrays = hp0[0] + hp1[0] + hp0[1] + hp1[1]
            terms[it, 2 * t, rows, :] = lanes(merge_all(arrays, lane, 8), natural)
            terms[it, 2 * t + 1, rows, :] = merge_all(hq0 + hq1, lane, 64)
            pair = pl.ds(2 * t, 2)
            copy(
                terms.at[it, pair], sterms.at[it, pair], ts_s.at[it], ts_r.at[it], band, sibling
            ).start()
            return carry

        lax.fori_loop(0, TILES, tile, 0)
        incoming = sterms.at[it]
        pltpu.make_async_copy(incoming, incoming, ts_r.at[it]).wait()

        def share(k):
            target = 2 * k + core
            out = jnp.zeros((ROWS, LANES), F32)
            for names, held in ((pv, terms), (spv, sterms)):
                for e in range(2 * TILES):
                    hit = jnp.where(names[e : e + 1, :] == target, 1.0, 0.0)
                    out = out + hit * held[it, e]
            return out

        def send_share(r, carry):
            k = peer_chip(CHIPS - r)
            sbuf[it, k] = share(k)
            copy(
                sbuf.at[it, k], rbuf.at[it, chip], rs_s.at[it], rs_r.at[it], band, 2 * k + core
            ).start()
            return carry

        lax.fori_loop(1, CHIPS, send_share, 0)
        rbuf[it, chip] = share(chip)
        all_of(rbuf.at[it], rs_r.at[it])
        normal = functools.reduce(lambda a, b: a + b, [rbuf[it, k] for k in range(CHIPS)])

        l = iota((SOLS, LANES), 1)
        part = l % BLOCK
        upper = (l & BLOCK) != 0
        packed = normal[SOLS:, :]
        outer_part = jnp.concatenate([packed, pltpu.roll(packed, 64, 1)], axis=0)
        per = scale[...]
        rho = pen[0:1, :]
        rhs = normal[:SOLS, :] * per + rho * (cons[...] - dual[...])
        h_diag = lanes(outer_part, jnp.where(upper, part, BLOCK + part)) * per + rho
        h_real = lanes(outer_part, 2 * BLOCK + part) * per
        h_imag = lanes(outer_part, 3 * BLOCK + part) * per
        determ = h_diag * lanes(h_diag, l ^ BLOCK) - h_real * h_real - h_imag * h_imag
        sign = jnp.where(upper == (l < 64), 1.0, -1.0)
        solved = (
            rhs * h_diag
            - lanes(rhs, l ^ BLOCK) * h_real
            + sign * lanes(rhs, l ^ (64 + BLOCK)) * h_imag
        ) / determ
        every[ITERS, core, chip] = solved
        total_of(it, solved + dual[...])
        return carry

    lax.fori_loop(0, ITERS, iteration, 0)

    gains = every[ITERS, core, chip]
    for k in range(8):
        gains_out[k] = gains[:, k * BLOCK : (k + 1) * BLOCK]
    coeff = coefficients(ITERS - 1, None)
    for k in range(8):
        coeff_out[k] = coeff[:NPOLY, k * BLOCK : (k + 1) * BLOCK]

    def sent(ref, sem):
        pltpu.make_async_copy(ref, ref, sem).wait()

    pairs_copy.wait_send()
    sums_copy.wait_send()
    sent(wrec.at[pl.ds(0, CHIPS - 1)], one.at[2])
    for it in range(ITERS):
        sent(every.at[it, 0, pl.ds(0, CHIPS - 1)], ag_s.at[it])
        sent(every.at[it, 0], sx_s.at[it])
        sent(terms.at[it], ts_s.at[it])
        sent(sbuf.at[it, pl.ds(0, CHIPS - 1)], rs_s.at[it])
        sent(prec.at[it, pl.ds(0, BANDS - 1)], ps_s.at[it])


def on_device(visibilities, model, start_gains, penalty, pairs, flags, chan_band):
    vmem, dma = pltpu.VMEM, pltpu.SemaphoreType.DMA
    block = (SOLS, LANES)
    gains, coeff = pl.pallas_call(
        kernel,
        out_shape=(
            jax.ShapeDtypeStruct((8, SOLS, BLOCK), F32),
            jax.ShapeDtypeStruct((8, NPOLY, BLOCK), F32),
        ),
        in_specs=[pl.BlockSpec(memory_space=pl.ANY)] * 7,
        out_specs=(pl.BlockSpec(memory_space=vmem), pl.BlockSpec(memory_space=vmem)),
        scratch_shapes=[
            vmem((8, TILES, CHANS, CELLS), BF16),
            vmem((8, TILES, CHANS, CELLS), BF16),
            vmem((8, SOLS, BLOCK), F32),
            vmem((1, BLOCK), F32),
            pltpu.SMEM((TILES, 2), jnp.int32),
            vmem((TILES, CELLS), jnp.int32),
            vmem((1, CHANS), jnp.int32),
            vmem((8, CHANS, CELLS), F32),
            vmem((8, CHANS, CELLS), F32),
            vmem((NCOEF, TILES, SOLS, CELLS), F32),
            vmem((ITERS + 1, 2, CHIPS, *block), F32),
            vmem((ITERS, 2 * TILES, ROWS, LANES), F32),
            vmem((ITERS, 2 * TILES, ROWS, LANES), F32),
            vmem((ITERS, CHIPS, ROWS, LANES), F32),
            vmem((ITERS, CHIPS, ROWS, LANES), F32),
            vmem((ITERS, BANDS, 32, LANES), F32),
            vmem((8, LANES), jnp.int32),
            vmem((8, LANES), jnp.int32),
            vmem((CHIPS, 8, LANES), F32),
            vmem((8, LANES), F32),
            vmem((8, LANES), F32),
            vmem((NPOLY, *block), F32),
            vmem(block, F32),
            vmem((8, LANES), F32),
            vmem(block, F32),
            vmem(block, F32),
            vmem((NPOLY, 16, LANES), F32),
            dma((7,)),
            *[dma((ITERS,))] * 10,
            dma((6,)),
        ],
        compiler_params=pltpu.CompilerParams(
            collective_id=0, has_side_effects=True, vmem_limit_bytes=40 * 1024 * 1024
        ),
        cost_estimate=pl.CostEstimate(
            flops=60_000_000, bytes_accessed=3_000_000, transcendentals=0
        ),
        name="admm",
    )(
        visibilities, model, start_gains, penalty.reshape(1, BLOCK), pairs, flags,
        chan_band.reshape(1, CHANS),
    )
    return gains, coeff


def solution(mesh):
    in_specs = (
        P(None, "base", "band", None),
        P(None, "base", "band", None),
        P(None, "band", "base"),
        P("base"),
        P("base", None),
        P("base", None),
        P("band"),
    )
    out_specs = (P(None, "band", "base"), P(None, None, "base"))
    return jax.shard_map(
        on_device, mesh=mesh, in_specs=in_specs, out_specs=out_specs, check_vma=False
    )
```

profile of v0, /device:TPU:0, one launch (start us, length us, event | category | flops | bytes accessed | tf_op | source)
XLA Modules:
  0.0 69.2 jit_solution(10707044597891141649)
XLA Ops:
  0.6 0.0 copy-start.2
  0.6 0.0 copy-start.3
  0.7 0.0 copy-start.4
  0.7 0.0 copy-start.5
  0.7 0.9 %copy.9.start_hbm = f32[8,32,16]{2,1,0:T(8,128)S(1)} copy(f32[8,32,16]{1,2,0:T(8,128)} %param.9) | data formatting | bytes 32768 | tf_op args[2]
  1.6 0.0 copy-done.2
  1.6 0.0 copy-done.3
  1.6 0.0 copy-done.4
  1.7 0.0 copy-done.5
  1.7 0.0 copy-start
  1.7 1.0 %copy-done = bf16[8,2,64,256]{3,2,1,0:T(8,128)(2,1)S(1)} copy-done((bf16[8,2,64,256]{3,2,1,0:T(8,128)(2,1)S(1)}, bf16[8,2,64,256]{3,2,1,0:T(8,128)(2,1)}, u32[]{:S(2)}) %copy-start) | copy-done | bytes 524312
  2.7 0.0 copy-start.1
  2.7 1.0 %copy-done.1 = bf16[8,2,64,256]{3,2,1,0:T(8,128)(2,1)S(1)} copy-done((bf16[8,2,64,256]{3,2,1,0:T(8,128)(2,1)S(1)}, bf16[8,2,64,256]{3,2,1,0:T(8,128)(2,1)}, u32[]{:S(2)}) %copy-start.1) | copy-done | bytes 524312
  3.8 64.1 %admm.1 = (f32[8,32,16]{2,1,0:T(8,128)S(1)}, f32[8,9,16]{2,1,0:T(8,128)S(1)}) custom-call(bf16[8,2,64,256]{3,2,1,0:T(8,128)(2,1)S(1)} %copy-done, bf16[8,2,64,256]{3,2,1,0:T(8,128)(2,1)S(1)} %copy-done.1, f32[8,32,16]{2,1,0:T(8,128)S(1)} %copy.9.start_hbm, f32[1,16]{1,0:T(1,128)S(1)} %bitcast.2, s32[2,2]{1,0:T(2,128)S(1)} %copy-done.3, ...), custom_call_target="tpu_custom_call" | custom-call | flops 60000000 | bytes 3000000 | tf_op jit(solution)/shard_map/admm/pallas_call | solution.py:513
  67.8 0.7 %copy.10 = f32[8,32,16]{1,2,0:T(8,128)} copy(f32[8,32,16]{2,1,0:T(8,128)S(1)} %get-tuple-element.2) | data formatting | bytes 32768 | tf_op jit(solution)/shard_map/admm/pallas_call | solution.py:513
  68.6 0.6 copy.11
Async XLA Ops:
  0.6 1.0 %copy-start.2 = (s32[2,256]{1,0:T(2,128)S(1)}, s32[2,256]{1,0:T(2,128)}, u32[]{:S(2)}) copy-start(s32[2,256]{1,0:T(2,128)} %flags_hbm.1) | copy-start | bytes 6148
  0.6 1.0 %copy-start.3 = (s32[2,2]{1,0:T(2,128)S(1)}, s32[2,2]{1,0:T(2,128)}, u32[]{:S(2)}) copy-start(s32[2,2]{1,0:T(2,128)} %pairs_hbm.1) | copy-start | bytes 52
  0.7 1.0 %copy-start.4 = (f32[16]{0:T(128)S(1)}, f32[16]{0:T(128)}, u32[]{:S(2)}) copy-start(f32[16]{0:T(128)} %param.10) | copy-start | bytes 196
  0.7 1.0 %copy-start.5 = (s32[64]{0:T(128)S(1)}, s32[64]{0:T(128)}, u32[]{:S(2)}) copy-start(s32[64]{0:T(128)} %param.13) | copy-start | bytes 772
  1.7 1.0 %copy-start = (bf16[8,2,64,256]{3,2,1,0:T(8,128)(2,1)S(1)}, bf16[8,2,64,256]{3,2,1,0:T(8,128)(2,1)}, u32[]{:S(2)}) copy-start(bf16[8,2,64,256]{3,2,1,0:T(8,128)(2,1)} %vis_hbm.1) | copy-start | bytes 1572868
  2.7 1.0 %copy-start.1 = (bf16[8,2,64,256]{3,2,1,0:T(8,128)(2,1)S(1)}, bf16[8,2,64,256]{3,2,1,0:T(8,128)(2,1)}, u32[]{:S(2)}) copy-start(bf16[8,2,64,256]{3,2,1,0:T(8,128)(2,1)} %mdl_hbm.1) | copy-start | bytes 1572868
where the time goes:
time: 69.4 us; the launch traced here: 69.2 us
  Pallas kernels  64.1 us (92%)
  local copies, waits for them, and re-layouts  4.4 us (6%)
  between operations  0.72 us (1%)
    pallas_call x1, Pallas kernels, on_device(): pl.pallas_call(kernel, out_shape=(jax.ShapeDtypeStruct((8, SOLS, BLOCK),...  64.1 us
    unnamed x13, local copies, waits for them, and re-layouts  3.04 us

commit v1 on v0

v1 whole, which is shorter than its diff:
```python
import functools

import jax
import jax.numpy as jnp
from jax import lax
from jax.experimental import pallas as pl
from jax.experimental.pallas import tpu as pltpu
from jax.sharding import PartitionSpec as P

BLOCK = 16
NPOLY = 9
ITERS = 3
RIDGE = 0.5
MESH = pl.DeviceIdType.MESH
F32 = jnp.float32
BF16 = jnp.bfloat16
SIDE = 4
CHIPS = SIDE * SIDE
BANDS = 4
TILES = 2
CHANS = 64
CELLS = BLOCK * BLOCK
SOLS = 32
LANES = 128
HALF = SOLS // 2
ROWS = HALF + HALF // 2
FAR = sorted(
    [(dz, dx) for dz in range(SIDE) for dx in range(SIDE) if dz or dx],
    key=lambda d: -sum(min(n, SIDE - n) for n in d),
)
NCOEF = 48
PAIRS = [(0, 1), (0, 2), (0, 3), (1, 2), (1, 3), (2, 3)]


def lanes(x, idx):
    numbers = lax.GatherDimensionNumbers(
        offset_dims=(),
        collapsed_slice_dims=(1,),
        start_index_map=(1,),
        operand_batching_dims=(0,),
        start_indices_batching_dims=(0,),
    )
    return lax.gather(
        x, idx[..., None], numbers, (1, 1), mode=lax.GatherScatterMode.PROMISE_IN_BOUNDS
    )


def iota(shape, axis):
    return lax.broadcasted_iota(jnp.int32, shape, axis)


def merge(a, b, lane, bit):
    clear = (lane & bit) == 0
    return jnp.where(clear, a, b) + lanes(jnp.where(clear, b, a), lane ^ bit)


def merge_all(arrays, lane, top):
    bit = top
    while len(arrays) > 1:
        half = len(arrays) // 2
        arrays = [merge(a, b, lane, bit) for a, b in zip(arrays[:half], arrays[half:])]
        bit //= 2
    return arrays[0]


def mul(a, b):
    return (a[0] * b[0] - a[1] * b[1], a[0] * b[1] + a[1] * b[0])


def mul_conj(a, b):
    return (a[0] * b[0] + a[1] * b[1], a[0] * b[1] - a[1] * b[0])


def conj(a):
    return (a[0], -a[1])


def add(*terms):
    re, im = terms[0]
    for t in terms[1:]:
        re, im = re + t[0], im + t[1]
    return (re, im)


def scaled(a, r):
    return (a[0] * r, a[1] * r)


def outer(j):
    c = [(j[k], j[4 + k]) for k in range(4)]
    q00 = c[0][0] * c[0][0] + c[0][1] * c[0][1] + c[2][0] * c[2][0] + c[2][1] * c[2][1]
    q11 = c[1][0] * c[1][0] + c[1][1] * c[1][1] + c[3][0] * c[3][0] + c[3][1] * c[3][1]
    q01 = add(mul_conj(c[0], c[1]), mul_conj(c[2], c[3]))
    return q00, q11, q01


def station_terms(load, jp, jq):
    p = [(jp[k], jp[4 + k]) for k in range(4)]
    q = [(jq[k], jq[4 + k]) for k in range(4)]
    cross = {}
    for ab in range(4):
        for cd in range(4):
            cross[ab, cd] = (load(4 * ab + cd), load(16 + 4 * ab + cd))
    gp, gq = [], []
    for a in range(2):
        for d in range(2):
            gp.append(
                add(
                    *[
                        mul(cross[2 * a + b, 2 * d + c], q[2 * b + c])
                        for b in range(2)
                        for c in range(2)
                    ]
                )
            )
            gq.append(
                add(
                    *[
                        mul_conj(cross[2 * b + a, 2 * c + d], p[2 * b + c])
                        for b in range(2)
                        for c in range(2)
                    ]
                )
            )
    diag = [load(32 + k) for k in range(4)]
    off = {pair: (load(36 + 2 * n), load(37 + 2 * n)) for n, pair in enumerate(PAIRS)}
    q00, q11, q01 = outer(jq)
    two = scaled(q01, 2.0)
    hp = [
        diag[0] * q00 + diag[1] * q11 + mul_conj(conj(off[0, 1]), two)[0],
        diag[2] * q00 + diag[3] * q11 + mul_conj(conj(off[2, 3]), two)[0],
        *add(
            scaled(off[0, 2], q00),
            mul(off[0, 3], q01),
            mul_conj(q01, off[1, 2]),
            scaled(off[1, 3], q11),
        ),
    ]
    r00, r11, r01 = outer(jp)
    two = scaled(r01, 2.0)
    hq = [
        diag[0] * r00 + diag[2] * r11 + mul_conj(off[0, 2], two)[0],
        diag[1] * r00 + diag[3] * r11 + mul_conj(off[1, 3], two)[0],
        *add(
            scaled(conj(off[0, 1]), r00),
            mul_conj(off[0, 3], r01),
            mul_conj(r01, off[1, 2]),
            scaled(conj(off[2, 3]), r11),
        ),
    ]
    gp = [g[0] for g in gp] + [g[1] for g in gp]
    gq = [g[0] for g in gq] + [g[1] for g in gq]
    return gp, hp, gq, hq


def kernel(
    vis_hbm, mdl_hbm, start_hbm, pen_hbm, pairs_hbm, flags_hbm, chan_hbm,
    gains_out, coeff_out,
    vis, mdl, start, pen_in, pairs, flags, chan, ends,
    vf, mf, coef, half_out, mine, every, terms, sbuf, rbuf, prec, names, away, wsend, wrec,
    solved_now, final, basis, scale, pen, cons, dual, ginv,
    loc, ag_s, ag_r, rs_s, rs_r, ps_s, ps_r, one,
):
    band = lax.axis_index("band")
    base = lax.axis_index("base")
    core = base % 2
    chip = base // 2
    cz = chip // SIDE
    cx = chip % SIDE
    sibling = chip * 2 + (1 - core)

    def at(dz, dx):
        return ((cz + dz) % SIDE) * SIDE + (cx + dx) % SIDE

    def copy(src, dst, send, recv, band_to, base_to):
        return pltpu.make_async_remote_copy(
            src_ref=src, dst_ref=dst, send_sem=send, recv_sem=recv,
            device_id=(band_to, base_to), device_id_type=MESH,
        )

    local = [
        pltpu.make_async_copy(src, dst, loc.at[n])
        for n, (src, dst) in enumerate(
            [
                (start_hbm, start), (pairs_hbm, pairs), (flags_hbm, flags), (chan_hbm, chan),
                (pen_hbm, pen_in), (mdl_hbm, mdl), (vis_hbm, vis),
            ]
        )
    ]
    for c in local:
        c.start()

    barrier = pltpu.get_barrier_semaphore()

    def greet(band_to, base_to):
        pl.semaphore_signal(barrier, inc=1, device_id=(band_to, base_to), device_id_type=MESH)

    for dz, dx in FAR:
        for c in range(2):
            greet(band, 2 * at(dz, dx) + c)
    for d in (2, 1, 3):
        for c in range(2):
            greet((band + d) % BANDS, 2 * chip + c)
    greet(band, sibling)

    lane8 = iota((8, LANES), 1)
    row8 = iota((8, LANES), 0)
    for c in local[:5]:
        c.wait()
    mine[...] = start[...].reshape(8 * BLOCK, SOLS).T
    keep = pl.ds(pl.multiple_of(core * HALF, HALF), HALF)
    give = pl.ds(pl.multiple_of((1 - core) * HALF, HALF), HALF)
    every[0, base] = mine[keep, :]

    for t in range(TILES):
        for side in range(2):
            ends[t, side] = pairs[t, side]
    blocks = [pairs[t, side] for t in range(TILES) for side in range(2)]
    named = jnp.zeros((8, LANES), jnp.int32)
    for e, b in enumerate(blocks):
        named = jnp.where(row8 == e, b, named)
    names[0] = named
    cell = iota((1, CELLS), 1)
    eye = (cell // BLOCK == cell % BLOCK).astype(F32)
    weights = []
    for t in range(TILES):
        same = jnp.where(blocks[2 * t] == blocks[2 * t + 1], 1.0, 0.0)
        weights.append(flags[t : t + 1, :].astype(F32) * (1.0 - same * eye))
    both = jnp.concatenate([*weights, jnp.zeros((6, CELLS), F32)], axis=0).astype(BF16)
    fold_row = iota((CELLS, LANES), 0)
    fold_lane = iota((CELLS, LANES), 1) % BLOCK
    at_first = jnp.dot(
        both, (fold_row // BLOCK == fold_lane).astype(F32).astype(BF16),
        preferred_element_type=F32,
    )
    at_second = jnp.dot(
        both, (fold_row % BLOCK == fold_lane).astype(F32).astype(BF16),
        preferred_element_type=F32,
    )
    pen_row = jnp.concatenate([pen_in[...]] * 8, axis=1)
    away[0] = jnp.concatenate(
        [at_first[0:1], at_second[0:1], at_first[1:2], at_second[1:2], pen_row]
        + [jnp.zeros((3, LANES), F32)],
        axis=0,
    )

    pl.semaphore_wait(barrier, 2 * CHIPS - 1 + 2 * (BANDS - 1))

    for dz, dx in FAR:
        for c in range(2):
            copy(
                mine.at[pl.ds(HALF * c, HALF)], every.at[0, base], ag_s.at[0], ag_r.at[0],
                band, 2 * at(dz, dx) + c,
            ).start()
    copy(mine.at[give], every.at[0, base], ag_s.at[0], ag_r.at[0], band, sibling).start()
    names_copy = copy(names.at[0], names.at[1], one.at[0], one.at[1], band, sibling)
    away_copy = copy(away.at[0], away.at[1], one.at[2], one.at[3], band, sibling)
    names_copy.start()
    away_copy.start()

    row = iota((SOLS, CHANS), 0)
    sol = band * SOLS + ((row // HALF + core) % 2) * HALF + row % HALF
    member = (jnp.broadcast_to(chan[...], (SOLS, CHANS)) == sol).astype(F32)
    where_c = (band * CHANS + iota((SOLS, CHANS), 1)).astype(F32)
    xpos = -1.0 + (2.0 * where_c + 1.0) / (CHANS * BANDS)
    chans = jnp.sum(member, axis=1, keepdims=True)
    centre = jnp.sum(member * xpos, axis=1, keepdims=True) / chans
    centre = jnp.broadcast_to(centre[:HALF], (HALF, LANES))
    cheb = [jnp.ones_like(centre), centre]
    for _ in range(2, NPOLY):
        cheb.append(2.0 * centre * cheb[-1] - cheb[-2])
    for k in range(NPOLY):
        basis[k] = cheb[k]
    member2 = jnp.concatenate([member, member], axis=1).astype(BF16)

    for c in local[5:]:
        c.wait()

    def collapse(t, carry):
        w = jnp.where(t == 0, weights[0], weights[1])
        for k in range(8):
            vf[k] = vis[k, t].astype(F32)
            mf[k] = mdl[k, t].astype(F32) * w

        def put(n, product):
            high = product.astype(BF16)
            low = (product - high.astype(F32)).astype(BF16)
            out = jnp.dot(
                member2, jnp.concatenate([high, low], axis=0), preferred_element_type=F32
            )
            coef[t, n] = out[:HALF]
            half_out[t, n] = out[HALF:]

        for ab in range(4):
            vr, vi = vf[ab], vf[4 + ab]
            for cd in range(4):
                mr, mi = mf[cd], mf[4 + cd]
                put(4 * ab + cd, vr * mr + vi * mi)
                put(16 + 4 * ab + cd, vi * mr - vr * mi)
        for ab in range(4):
            put(32 + ab, mf[ab] * mf[ab] + mf[4 + ab] * mf[4 + ab])
        for n, (x, y) in enumerate(PAIRS):
            put(36 + 2 * n, mf[x] * mf[y] + mf[4 + x] * mf[4 + y])
            put(37 + 2 * n, mf[4 + x] * mf[y] - mf[x] * mf[4 + y])
        copy(half_out.at[t], coef.at[TILES + t], one.at[4], one.at[5], band, sibling).start()
        return carry

    lax.fori_loop(0, TILES, collapse, 0)

    names_copy.wait_recv()
    away_copy.wait_recv()
    for t in range(TILES):
        for side in range(2):
            ends[TILES + t, side] = names[1, 2 * t + side, 0]

    def weight_rows(k):
        out = jnp.zeros((8, LANES), F32)
        for own in range(2):
            for e in range(2 * TILES):
                hit = row8 + 2 * k == names[own, e : e + 1, :]
                at_end = jnp.broadcast_to(away[own, e : e + 1, :], (8, LANES))
                out = out + jnp.where(hit, at_end, 0.0)
        return out

    for dz, dx in FAR:
        k = at(dz, dx)
        wsend[k] = weight_rows(k)
        copy(
            wsend.at[k], wrec.at[chip], one.at[6], one.at[7], band, 2 * k + core
        ).start()
    wrec[chip] = weight_rows(chip)
    own_pen = jnp.broadcast_to(away[0, 4:5, :], (HALF, LANES))
    its_pen = jnp.broadcast_to(away[1, 4:5, :], (HALF, LANES))
    pen[0] = jnp.where(core == 0, own_pen, its_pen)
    pen[1] = jnp.where(core == 0, its_pen, own_pen)

    def arrived(ref, sem):
        pltpu.make_async_copy(ref, ref, sem).wait()

    arrived(half_out, one.at[5])

    def total_of(it, values):
        lane = iota((HALF, LANES), 1)
        columns = jnp.zeros((HALF, LANES), F32)
        for k in range(NPOLY):
            columns = jnp.where(lane == k, basis[k], columns)
        pad = [jnp.zeros((16 - NPOLY, LANES), F32)]
        out = []
        for part in (values[0], values[1], columns):
            out += [jnp.sum(basis[k] * part, axis=0, keepdims=True) for k in range(NPOLY)] + pad
        me = 2 * band + core
        prec[it, me] = jnp.concatenate(out, axis=0)

        def send(band_to, base_to):
            copy(
                prec.at[it, me], prec.at[it, me], ps_s.at[it], ps_r.at[it], band_to, base_to
            ).start()

        for d in (2, 1, 3):
            for c in range(2):
                send((band + d) % BANDS, 2 * chip + c)
        send(band, sibling)

    def coefficients(it, first):
        arrived(prec.at[it, pl.ds(0, 2 * BANDS - 1)], ps_r.at[it])
        total = functools.reduce(lambda a, b: a + b, [prec[it, k] for k in range(2 * BANDS)])

        def invert():
            r, l = iota((16, LANES), 0), iota((16, LANES), 1)
            m = total[32:, :] + jnp.where((r == l) & (r < NPOLY), RIDGE, 0.0)
            m = m + jnp.where((l == r + 16) & (r < NPOLY), 1.0, 0.0)
            for p in range(NPOLY):
                pivot = m[p : p + 1, :] / m[p : p + 1, p : p + 1]
                m = jnp.where(r == p, pivot, m - m[:, p : p + 1] * pivot)
            for k in range(NPOLY):
                ginv[k] = jnp.broadcast_to(m[:, 16 + k : 17 + k], (16, LANES))

        if first is not None:
            pl.when(first)(invert)
        out = []
        for b in range(2):
            rhs = total[16 * b : 16 * b + 16, :]
            x = ginv[0] * rhs[0:1, :]
            for k in range(1, NPOLY):
                x = x + ginv[k] * rhs[k : k + 1, :]
            out.append(x)
        return out

    lane = iota((HALF, LANES), 1)
    inner = lane % BLOCK

    def natural(l):
        return (l % 8) * BLOCK + ((l % BLOCK) // 8) * 8 + l // BLOCK

    own_blocks = pl.ds(2 * chip, 2)

    def iteration(it, carry):
        @pl.when(it > 0)
        def _():
            every[it, own_blocks] = solved_now[...]
            for dz, dx in FAR:
                copy(
                    every.at[it, own_blocks], every.at[it, own_blocks], ag_s.at[it], ag_r.at[it],
                    band, 2 * at(dz, dx) + core,
                ).start()
            coeff = coefficients(it - 1, it == 1)
            for b in range(2):
                agreed = basis[0] * coeff[b][0:1, :]
                for k in range(1, NPOLY):
                    agreed = agreed + basis[k] * coeff[b][k : k + 1, :]
                dual[b] = dual[b] + solved_now[b] - agreed
                cons[b] = agreed
            arrived(every.at[it, pl.ds(0, 2 * CHIPS - 2)], ag_r.at[it])

        @pl.when(it == 0)
        def _():
            arrived(every.at[0, pl.ds(0, 2 * CHIPS - 1)], ag_r.at[0])
            cons[...] = every[0, own_blocks]
            dual[...] = jnp.zeros((2, HALF, LANES), F32)

        def tile(t, carry):
            of_p = every[it, ends[t, 0]]
            of_q = every[it, ends[t, 1]]
            jq = [lanes(of_q, k * BLOCK + inner) for k in range(8)]
            gp, hp, gq, hq = [], [], [], []
            for half in range(2):
                jp = [lanes(of_p, k * BLOCK + half * 8 + lane // BLOCK) for k in range(8)]

                def load(n):
                    return coef[t, n, :, pl.ds(half * LANES, LANES)]

                a, b, c, d = station_terms(load, jp, jq)
                gp += a
                hp += b
                gq.append(c)
                hq.append(d)
            terms[2 * t, pl.ds(0, HALF), :] = lanes(merge_all(gp, lane, 8), natural(lane))
            summed = [x + y for x, y in zip(gq[0], gq[1])]
            terms[2 * t + 1, pl.ds(0, HALF), :] = merge_all(summed, lane, 64)
            summed = [x + y for x, y in zip(hq[0], hq[1])]
            rows = pl.ds(HALF, 8)
            arrays = [x[:8] for x in hp[:4]] + [x[8:] for x in hp[:4]]
            arrays += [x[:8] for x in hp[4:]] + [x[8:] for x in hp[4:]]
            terms[2 * t, rows, :] = lanes(merge_all(arrays, lane8, 8), natural(lane8))
            arrays = [x[:8] for x in summed] + [x[8:] for x in summed]
            terms[2 * t + 1, rows, :] = merge_all(arrays, lane8, 64)
            return carry

        lax.fori_loop(0, 2 * TILES, tile, 0)

        def share(k):
            out = [jnp.zeros((ROWS, LANES), F32) for _ in range(2)]
            for own in range(2):
                for e in range(2 * TILES):
                    held = terms[2 * TILES * own + e]
                    for b in range(2):
                        hit = jnp.where(names[own, e : e + 1, :] == 2 * k + b, 1.0, 0.0)
                        out[b] = out[b] + hit * held
            return out

        for dz, dx in FAR:
            k = at(dz, dx)
            out = share(k)
            sbuf[it, k, 0] = out[0]
            sbuf[it, k, 1] = out[1]
            copy(
                sbuf.at[it, k], rbuf.at[it, chip], rs_s.at[it], rs_r.at[it], band, 2 * k + core
            ).start()
        out = share(chip)
        rbuf[it, chip, 0] = out[0]
        rbuf[it, chip, 1] = out[1]

        @pl.when(it == 0)
        def _():
            arrived(wrec.at[pl.ds(0, CHIPS - 1)], one.at[7])
            total = functools.reduce(lambda a, b: a + b, [wrec[k] for k in range(CHIPS)])
            for b in range(2):
                at_station = jnp.broadcast_to(total[b : b + 1, :], (HALF, LANES))
                scale[b] = 1.0 / jnp.maximum(chans[:HALF] * at_station, 1.0)

        arrived(rbuf.at[it, pl.ds(0, CHIPS - 1)], rs_r.at[it])

        part = lane % BLOCK
        upper = (lane & BLOCK) != 0
        sign = jnp.where(upper == (lane < 64), 1.0, -1.0)
        result = []
        for b in range(2):
            normal = functools.reduce(lambda x, y: x + y, [rbuf[it, k, b] for k in range(CHIPS)])
            packed = normal[HALF:, :]
            outer_part = jnp.concatenate([packed, pltpu.roll(packed, 64, 1)], axis=0)
            per = scale[b]
            rho = pen[b]
            rhs = normal[:HALF, :] * per + rho * (cons[b] - dual[b])
            h_diag = lanes(outer_part, jnp.where(upper, part, BLOCK + part)) * per + rho
            h_real = lanes(outer_part, 2 * BLOCK + part) * per
            h_imag = lanes(outer_part, 3 * BLOCK + part) * per
            determ = h_diag * lanes(h_diag, lane ^ BLOCK) - h_real * h_real - h_imag * h_imag
            solved = (
                rhs * h_diag
                - lanes(rhs, lane ^ BLOCK) * h_real
                + sign * lanes(rhs, lane ^ (64 + BLOCK)) * h_imag
            ) / determ
            solved_now[b] = solved
            result.append(solved + dual[b])
        total_of(it, result)
        return carry

    lax.fori_loop(0, ITERS, iteration, 0)

    final_copy = copy(
        solved_now.at[1 - core], final.at[core], one.at[8], one.at[9], band, sibling
    )
    final_copy.start()
    final[core] = solved_now[core]
    final_copy.wait_recv()
    gains = jnp.concatenate([final[0], final[1]], axis=0)
    for k in range(8):
        gains_out[k] = gains[:, k * BLOCK : (k + 1) * BLOCK]
    pair = coefficients(ITERS - 1, None)
    coeff = jnp.where(core == 0, pair[0], pair[1])
    for k in range(8):
        coeff_out[k] = coeff[:NPOLY, k * BLOCK : (k + 1) * BLOCK]

    names_copy.wait_send()
    away_copy.wait_send()
    final_copy.wait_send()
    arrived(half_out, one.at[4])
    arrived(wsend.at[pl.ds(0, CHIPS - 1)], one.at[6])
    arrived(every.at[0, pl.ds(0, 2 * CHIPS - 1)], ag_s.at[0])
    for it in range(ITERS):
        if it > 0:
            arrived(every.at[it, pl.ds(0, 2 * CHIPS - 2)], ag_s.at[it])
        arrived(sbuf.at[it, pl.ds(0, CHIPS - 1)], rs_s.at[it])
        arrived(prec.at[it, pl.ds(0, 2 * BANDS - 1)], ps_s.at[it])


def on_device(visibilities, model, start_gains, penalty, pairs, flags, chan_band):
    vmem, dma = pltpu.VMEM, pltpu.SemaphoreType.DMA
    gains, coeff = pl.pallas_call(
        kernel,
        out_shape=(
            jax.ShapeDtypeStruct((8, SOLS, BLOCK), F32),
            jax.ShapeDtypeStruct((8, NPOLY, BLOCK), F32),
        ),
        in_specs=[pl.BlockSpec(memory_space=pltpu.HBM)] * 7,
        out_specs=(pl.BlockSpec(memory_space=vmem), pl.BlockSpec(memory_space=vmem)),
        scratch_shapes=[
            vmem((8, TILES, CHANS, CELLS), BF16),
            vmem((8, TILES, CHANS, CELLS), BF16),
            vmem((8, BLOCK, SOLS), F32),
            vmem((1, BLOCK), F32),
            pltpu.SMEM((TILES, 2), jnp.int32),
            vmem((TILES, CELLS), jnp.int32),
            vmem((1, CHANS), jnp.int32),
            pltpu.SMEM((2 * TILES, 2), jnp.int32),
            vmem((8, CHANS, CELLS), F32),
            vmem((8, CHANS, CELLS), F32),
            vmem((2 * TILES, NCOEF, HALF, CELLS), F32),
            vmem((TILES, NCOEF, HALF, CELLS), F32),
            vmem((SOLS, LANES), F32),
            vmem((ITERS, 2 * CHIPS, HALF, LANES), F32),
            vmem((4 * TILES, ROWS, LANES), F32),
            vmem((ITERS, CHIPS, 2, ROWS, LANES), F32),
            vmem((ITERS, CHIPS, 2, ROWS, LANES), F32),
            vmem((ITERS, 2 * BANDS, 48, LANES), F32),
            vmem((2, 8, LANES), jnp.int32),
            vmem((2, 8, LANES), F32),
            vmem((CHIPS, 8, LANES), F32),
            vmem((CHIPS, 8, LANES), F32),
            vmem((2, HALF, LANES), F32),
            vmem((2, HALF, LANES), F32),
            vmem((NPOLY, HALF, LANES), F32),
            vmem((2, HALF, LANES), F32),
            vmem((2, HALF, LANES), F32),
            vmem((2, HALF, LANES), F32),
            vmem((2, HALF, LANES), F32),
            vmem((NPOLY, 16, LANES), F32),
            dma((7,)),
            *[dma((ITERS,))] * 6,
            dma((10,)),
        ],
        compiler_params=pltpu.CompilerParams(
            collective_id=0, has_side_effects=True, vmem_limit_bytes=40 * 1024 * 1024
        ),
        cost_estimate=pl.CostEstimate(
            flops=60_000_000, bytes_accessed=3_000_000, transcendentals=0
        ),
        name="admm",
    )(
        visibilities, model, jnp.swapaxes(start_gains, 1, 2), penalty.reshape(1, BLOCK), pairs, flags,
        chan_band.reshape(1, CHANS),
    )
    return gains, coeff


def solution(mesh):
    in_specs = (
        P(None, "base", "band", None),
        P(None, "base", "band", None),
        P(None, "band", "base"),
        P("base"),
        P("base", None),
        P("base", None),
        P("band"),
    )
    out_specs = (P(None, "band", "base"), P(None, None, "base"))
    return jax.shard_map(
        on_device, mesh=mesh, in_specs=in_specs, out_specs=out_specs, check_vma=False
    )
```

time: 69.4 us -> 63.4 us (0.914)
  the two profiles are of different devices: /device:TPU:0 before, /device:TPU:1 now
where the time goes in v1:
time: 63.4 us; the launch traced here: 63.1 us
  Pallas kernels  57.5 us (91%)
  local copies, waits for them, and re-layouts  4.96 us (8%)
  between operations  0.68 us (1%)
    pallas_call x1, Pallas kernels, on_device(): pl.pallas_call(kernel, out_shape=(jax.ShapeDtypeStruct((8, SOLS, BLOCK),...  57.5 us
    unnamed x14, local copies, waits for them, and re-layouts  3.6 us
    pallas_call x2, local copies, waits for them, and re-layouts, on_device(): pl.pallas_call(kernel, out_shape=(jax.ShapeDtypeStruct((8, SOLS, BLOCK),...  1.36 us

profile of v1, /device:TPU:1, one launch (start us, length us, event | category | flops | bytes accessed | tf_op | source)
XLA Modules:
  0.0 63.1 jit_solution(6719196824363948175)
XLA Ops:
  0.6 0.0 copy-start.6
  0.6 0.0 copy-start.3
  0.7 0.0 copy-start.4
  0.7 0.0 copy-start.5
  0.7 0.6 copy-done.6
  1.3 0.0 copy-done.3
  1.3 0.0 copy-done.4
  1.3 0.0 copy-done.5
  1.3 0.0 copy-start
  1.3 1.0 %copy-done = bf16[8,2,64,256]{3,2,1,0:T(8,128)(2,1)S(1)} copy-done((bf16[8,2,64,256]{3,2,1,0:T(8,128)(2,1)S(1)}, bf16[8,2,64,256]{3,2,1,0:T(8,128)(2,1)}, u32[]{:S(2)}) %copy-start) | copy-done | bytes 524312
  2.4 0.0 copy-start.1
  2.4 1.0 %copy-done.1 = bf16[8,2,64,256]{3,2,1,0:T(8,128)(2,1)S(1)} copy-done((bf16[8,2,64,256]{3,2,1,0:T(8,128)(2,1)S(1)}, bf16[8,2,64,256]{3,2,1,0:T(8,128)(2,1)}, u32[]{:S(2)}) %copy-start.1) | copy-done | bytes 524312
  3.4 0.0 copy-start.2
  3.4 0.8 %copy-done.2 = f32[8,32,16]{1,2,0:T(8,128)S(1)} copy-done((f32[8,32,16]{1,2,0:T(8,128)S(1)}, f32[8,32,16]{1,2,0:T(8,128)}, u32[]{:S(2)}) %copy-start.2) | copy-done | bytes 16408
  4.3 57.5 %admm.1 = (f32[8,32,16]{2,1,0:T(8,128)S(1)}, f32[8,9,16]{2,1,0:T(8,128)S(1)}) custom-call(bf16[8,2,64,256]{3,2,1,0:T(8,128)(2,1)S(1)} %copy-done, bf16[8,2,64,256]{3,2,1,0:T(8,128)(2,1)S(1)} %copy-done.1, f32[8,16,32]{2,1,0:T(8,128)S(1)} %bitcast.3, f32[1,16]{1,0:T(1,128)S(1)} %bitcast.4, s32[2,2]{1,0:T(2,128)S(1)} %copy-done.4, s32[2,256]{1,0:T(2,128)S(1)} %copy-done.3, ...), custom_call_target="tpu_custom_call" | custom-call | flops 60000000 | bytes 3000000 | tf_op jit(solution)/shard_map/admm/pallas_call | solution.py:539
  61.8 0.7 %copy.9 = f32[8,32,16]{1,2,0:T(8,128)} copy(f32[8,32,16]{2,1,0:T(8,128)S(1)} %get-tuple-element.2) | data formatting | bytes 32768 | tf_op jit(solution)/shard_map/admm/pallas_call | solution.py:539
  62.5 0.6 copy.10
Async XLA Ops:
  0.6 0.7 %copy-start.6 = (s32[64]{0:T(128)S(1)}, s32[64]{0:T(128)}, u32[]{:S(2)}) copy-start(s32[64]{0:T(128)} %param.13) | copy-start | bytes 772
  0.6 0.7 %copy-start.3 = (s32[2,256]{1,0:T(2,128)S(1)}, s32[2,256]{1,0:T(2,128)}, u32[]{:S(2)}) copy-start(s32[2,256]{1,0:T(2,128)} %flags_hbm.1) | copy-start | bytes 6148
  0.7 0.7 %copy-start.4 = (s32[2,2]{1,0:T(2,128)S(1)}, s32[2,2]{1,0:T(2,128)}, u32[]{:S(2)}) copy-start(s32[2,2]{1,0:T(2,128)} %pairs_hbm.1) | copy-start | bytes 52
  0.7 0.7 %copy-start.5 = (f32[16]{0:T(128)S(1)}, f32[16]{0:T(128)}, u32[]{:S(2)}) copy-start(f32[16]{0:T(128)} %param.10) | copy-start | bytes 196
  1.3 1.0 %copy-start = (bf16[8,2,64,256]{3,2,1,0:T(8,128)(2,1)S(1)}, bf16[8,2,64,256]{3,2,1,0:T(8,128)(2,1)}, u32[]{:S(2)}) copy-start(bf16[8,2,64,256]{3,2,1,0:T(8,128)(2,1)} %vis_hbm.1) | copy-start | bytes 1572868
  2.4 1.0 %copy-start.1 = (bf16[8,2,64,256]{3,2,1,0:T(8,128)(2,1)S(1)}, bf16[8,2,64,256]{3,2,1,0:T(8,128)(2,1)}, u32[]{:S(2)}) copy-start(bf16[8,2,64,256]{3,2,1,0:T(8,128)(2,1)} %mdl_hbm.1) | copy-start | bytes 1572868
  3.4 0.8 %copy-start.2 = (f32[8,32,16]{1,2,0:T(8,128)S(1)}, f32[8,32,16]{1,2,0:T(8,128)}, u32[]{:S(2)}) copy-start(f32[8,32,16]{1,2,0:T(8,128)} %param.9) | copy-start | bytes 49156

commit v2 on v1

--- a/solution.py
+++ b/solution.py
@@ -158,7 +158,7 @@
     gains_out, coeff_out,
     vis, mdl, start, pen_in, pairs, flags, chan, ends,
     vf, mf, coef, half_out, mine, every, terms, sbuf, rbuf, prec, names, away, wsend, wrec,
-    solved_now, final, basis, scale, pen, cons, dual, ginv,
+    mixed, final, last, basis, scale, pen, cons, dual, ginv,
     loc, ag_s, ag_r, rs_s, rs_r, ps_s, ps_r, one,
 ):
     band = lax.axis_index("band")
@@ -339,16 +339,18 @@
 
     arrived(half_out, one.at[5])
 
-    def total_of(it, values):
-        lane = iota((HALF, LANES), 1)
+    pad = [jnp.zeros((16 - NPOLY, LANES), F32)]
+    me = 2 * band + core
+
+    def along_basis(part):
+        return [jnp.sum(basis[k] * part, axis=0, keepdims=True) for k in range(NPOLY)] + pad
+
+    def total_of(it):
+        column = iota((HALF, LANES), 1)
         columns = jnp.zeros((HALF, LANES), F32)
         for k in range(NPOLY):
-            columns = jnp.where(lane == k, basis[k], columns)
-        pad = [jnp.zeros((16 - NPOLY, LANES), F32)]
-        out = []
-        for part in (values[0], values[1], columns):
-            out += [jnp.sum(basis[k] * part, axis=0, keepdims=True) for k in range(NPOLY)] + pad
-        me = 2 * band + core
+            columns = jnp.where(column == k, basis[k], columns)
+        out = along_basis(mixed[0]) + along_basis(mixed[1]) + along_basis(columns)
         prec[it, me] = jnp.concatenate(out, axis=0)
 
         def send(band_to, base_to):
@@ -361,11 +363,19 @@
                 send((band + d) % BANDS, 2 * chip + c)
         send(band, sibling)
 
-    def coefficients(it, first):
+    def total_at(it):
         arrived(prec.at[it, pl.ds(0, 2 * BANDS - 1)], ps_r.at[it])
-        total = functools.reduce(lambda a, b: a + b, [prec[it, k] for k in range(2 * BANDS)])
-
-        def invert():
+        return functools.reduce(lambda a, b: a + b, [prec[it, k] for k in range(2 * BANDS)])
+
+    def solve_gram(rhs):
+        x = ginv[0] * rhs[0:1, :]
+        for k in range(1, NPOLY):
+            x = x + ginv[k] * rhs[k : k + 1, :]
+        return x
+
+    def from_total(total, first):
+        @pl.when(first)
+        def _():
             r, l = iota((16, LANES), 0), iota((16, LANES), 1)
             m = total[32:, :] + jnp.where((r == l) & (r < NPOLY), RIDGE, 0.0)
             m = m + jnp.where((l == r + 16) & (r < NPOLY), 1.0, 0.0)
@@ -375,16 +385,7 @@
             for k in range(NPOLY):
                 ginv[k] = jnp.broadcast_to(m[:, 16 + k : 17 + k], (16, LANES))
 
-        if first is not None:
-            pl.when(first)(invert)
-        out = []
-        for b in range(2):
-            rhs = total[16 * b : 16 * b + 16, :]
-            x = ginv[0] * rhs[0:1, :]
-            for k in range(1, NPOLY):
-                x = x + ginv[k] * rhs[k : k + 1, :]
-            out.append(x)
-        return out
+        return [solve_gram(total[16 * b : 16 * b + 16, :]) for b in range(2)]
 
     lane = iota((HALF, LANES), 1)
     inner = lane % BLOCK
@@ -397,18 +398,12 @@
     def iteration(it, carry):
         @pl.when(it > 0)
         def _():
-            every[it, own_blocks] = solved_now[...]
-            for dz, dx in FAR:
-                copy(
-                    every.at[it, own_blocks], every.at[it, own_blocks], ag_s.at[it], ag_r.at[it],
-                    band, 2 * at(dz, dx) + core,
-                ).start()
-            coeff = coefficients(it - 1, it == 1)
+            coeff = from_total(total_at(it - 1), it == 1)
             for b in range(2):
                 agreed = basis[0] * coeff[b][0:1, :]
                 for k in range(1, NPOLY):
                     agreed = agreed + basis[k] * coeff[b][k : k + 1, :]
-                dual[b] = dual[b] + solved_now[b] - agreed
+                dual[b] = mixed[b] - agreed
                 cons[b] = agreed
             arrived(every.at[it, pl.ds(0, 2 * CHIPS - 2)], ag_r.at[it])
 
@@ -446,7 +441,7 @@
             terms[2 * t + 1, rows, :] = merge_all(arrays, lane8, 64)
             return carry
 
-        lax.fori_loop(0, 2 * TILES, tile, 0)
+        lax.fori_loop(0, 2 * TILES, tile, 0, unroll=2)
 
         def share(k):
             out = [jnp.zeros((ROWS, LANES), F32) for _ in range(2)]
@@ -500,26 +495,55 @@
                 - lanes(rhs, lane ^ BLOCK) * h_real
                 + sign * lanes(rhs, lane ^ (64 + BLOCK)) * h_imag
             ) / determ
-            solved_now[b] = solved
-            result.append(solved + dual[b])
-        total_of(it, result)
+            every[it + 1, 2 * chip + b] = solved
+            result.append(solved)
+
+        @pl.when(it + 1 < ITERS)
+        def _():
+            for dz, dx in FAR:
+                copy(
+                    every.at[it + 1, own_blocks], every.at[it + 1, own_blocks],
+                    ag_s.at[it + 1], ag_r.at[it + 1], band, 2 * at(dz, dx) + core,
+                ).start()
+
+        for b in range(2):
+            mixed[b] = result[b] + dual[b]
+
+        @pl.when(it + 1 < ITERS)
+        def _():
+            total_of(it)
+
         return carry
 
     lax.fori_loop(0, ITERS, iteration, 0)
 
+    for c in range(2):
+        last[c] = jnp.concatenate(along_basis(mixed[c]), axis=0)
+
+    def send_last(c, band_to, base_to):
+        copy(
+            last.at[c], last.at[2 + me], one.at[10], one.at[11], band_to, base_to
+        ).start()
+
+    for d in (2, 1, 3):
+        for c in range(2):
+            send_last(c, (band + d) % BANDS, 2 * chip + c)
+    send_last(1 - core, band, sibling)
     final_copy = copy(
-        solved_now.at[1 - core], final.at[core], one.at[8], one.at[9], band, sibling
+        every.at[ITERS, sibling], final.at[core], one.at[8], one.at[9], band, sibling
     )
     final_copy.start()
-    final[core] = solved_now[core]
+    last[2 + me] = last[core]
+    final[core] = every[ITERS, base]
     final_copy.wait_recv()
     gains = jnp.concatenate([final[0], final[1]], axis=0)
+    gains_out[...] = gains.T.reshape(8, BLOCK, SOLS)
+    arrived(last.at[pl.ds(0, 2 * BANDS - 1)], one.at[11])
+    coeff = solve_gram(
+        functools.reduce(lambda a, b: a + b, [last[2 + k] for k in range(2 * BANDS)])
+    )
     for k in range(8):
-        gains_out[k] = gains[:, k * BLOCK : (k + 1) * BLOCK]
-    pair = coefficients(ITERS - 1, None)
-    coeff = jnp.where(core == 0, pair[0], pair[1])
-    for k in range(8):
-        coeff_out[k] = coeff[:NPOLY, k * BLOCK : (k + 1) * BLOCK]
+        coeff_out[:, k, :] = coeff[:NPOLY, k * BLOCK : (k + 1) * BLOCK]
 
     names_copy.wait_send()
     away_copy.wait_send()
@@ -531,7 +555,9 @@
         if it > 0:
             arrived(every.at[it, pl.ds(0, 2 * CHIPS - 2)], ag_s.at[it])
         arrived(sbuf.at[it, pl.ds(0, CHIPS - 1)], rs_s.at[it])
-        arrived(prec.at[it, pl.ds(0, 2 * BANDS - 1)], ps_s.at[it])
+        if it + 1 < ITERS:
+            arrived(prec.at[it, pl.ds(0, 2 * BANDS - 1)], ps_s.at[it])
+    arrived(last.at[pl.ds(0, 2 * BANDS - 1)], one.at[10])
 
 
 def on_device(visibilities, model, start_gains, penalty, pairs, flags, chan_band):
@@ -539,8 +565,8 @@
     gains, coeff = pl.pallas_call(
         kernel,
         out_shape=(
-            jax.ShapeDtypeStruct((8, SOLS, BLOCK), F32),
-            jax.ShapeDtypeStruct((8, NPOLY, BLOCK), F32),
+            jax.ShapeDtypeStruct((8, BLOCK, SOLS), F32),
+            jax.ShapeDtypeStruct((NPOLY, 8, BLOCK), F32),
         ),
         in_specs=[pl.BlockSpec(memory_space=pltpu.HBM)] * 7,
         out_specs=(pl.BlockSpec(memory_space=vmem), pl.BlockSpec(memory_space=vmem)),
@@ -558,7 +584,7 @@
             vmem((2 * TILES, NCOEF, HALF, CELLS), F32),
             vmem((TILES, NCOEF, HALF, CELLS), F32),
             vmem((SOLS, LANES), F32),
-            vmem((ITERS, 2 * CHIPS, HALF, LANES), F32),
+            vmem((ITERS + 1, 2 * CHIPS, HALF, LANES), F32),
             vmem((4 * TILES, ROWS, LANES), F32),
             vmem((ITERS, CHIPS, 2, ROWS, LANES), F32),
             vmem((ITERS, CHIPS, 2, ROWS, LANES), F32),
@@ -569,6 +595,7 @@
             vmem((CHIPS, 8, LANES), F32),
             vmem((2, HALF, LANES), F32),
             vmem((2, HALF, LANES), F32),
+            vmem((2 + 2 * BANDS, 16, LANES), F32),
             vmem((NPOLY, HALF, LANES), F32),
             vmem((2, HALF, LANES), F32),
             vmem((2, HALF, LANES), F32),
@@ -577,10 +604,10 @@
             vmem((NPOLY, 16, LANES), F32),
             dma((7,)),
             *[dma((ITERS,))] * 6,
-            dma((10,)),
+            dma((12,)),
         ],
         compiler_params=pltpu.CompilerParams(
-            collective_id=0, has_side_effects=True, vmem_limit_bytes=40 * 1024 * 1024
+            collective_id=0, has_side_effects=True, vmem_limit_bytes=60 * 1024 * 1024
         ),
         cost_estimate=pl.CostEstimate(
             flops=60_000_000, bytes_accessed=3_000_000, transcendentals=0
@@ -590,7 +617,7 @@
         visibilities, model, jnp.swapaxes(start_gains, 1, 2), penalty.reshape(1, BLOCK), pairs, flags,
         chan_band.reshape(1, CHANS),
     )
-    return gains, coeff
+    return jnp.swapaxes(gains, 1, 2), jnp.swapaxes(coeff, 0, 1)
 
 
 def solution(mesh):

time: 63.4 us -> 59.7 us (0.942)
  local copies, waits for them, and re-layouts: 4.96 us -> 2.1 us
  Pallas kernels: 57.5 us -> 56.8 us
    unnamed x14 -> x4, local copies, waits for them, and re-layouts: 3.6 us -> 2.1 us
    pallas_call x2 -> x0, local copies, waits for them, and re-layouts: 1.36 us -> none  [on_device(): pl.pallas_call(kernel, out_shape=(jax.ShapeDtypeStruct((8, SOLS, BLOCK),...]
    pallas_call x1, Pallas kernels: 57.5 us -> 56.8 us  [on_device(): pl.pallas_call(kernel, out_shape=(jax.ShapeDtypeStruct((8, BLOCK, SOLS),...]
where the time goes in v2:
time: 59.7 us; the launch traced here: 59.5 us
  Pallas kernels  56.8 us (95%)
  local copies, waits for them, and re-layouts  2.1 us (4%)
  between operations  0.65 us (1%)
    pallas_call x1, Pallas kernels, on_device(): pl.pallas_call(kernel, out_shape=(jax.ShapeDtypeStruct((8, BLOCK, SOLS),...  56.8 us
    unnamed x4, local copies, waits for them, and re-layouts  2.1 us

profile of v2, /device:TPU:1, one launch (start us, length us, event | category | flops | bytes accessed | tf_op | source)
XLA Modules:
  0.0 59.5 jit_solution(15769429835889970839)
XLA Ops:
  0.6 56.8 %admm.1 = (f32[8,16,32]{2,1,0:T(8,128)}, f32[9,8,16]{2,1,0:T(8,128)}) custom-call(bf16[8,2,64,256]{3,2,1,0:T(8,128)(2,1)} %vis_hbm.1, bf16[8,2,64,256]{3,2,1,0:T(8,128)(2,1)} %mdl_hbm.1, f32[8,16,32]{2,1,0:T(8,128)} %bitcast.5, f32[1,16]{1,0:T(1,128)} %bitcast.8, s32[2,2]{1,0:T(2,128)} %pairs_hbm.1, s32[2,256]{1,0:T(2,128)} %flags_hbm.1, s32[1,64]{1,0:T(1,128)} %bitcast.9), custom_call_target="tpu_custom_call" | custom-call | flops 60000000 | bytes 3000000 | tf_op jit(solution)/shard_map/admm/pallas_call | solution.py:565
  57.4 0.0 copy-start
  57.4 1.5 %copy.11 = f32[8,32,16]{1,2,0:T(8,128)} copy(f32[8,32,16]{1,2,0:T(8,128)} %bitcast.6) | data formatting | bytes 32768
  58.9 0.0 copy-done
  58.9 0.6 %copy.12 = f32[8,9,16]{2,0,1:T(8,128)} copy(f32[8,9,16]{2,0,1:T(8,128)S(1)} %bitcast.7) | data formatting | bytes 9216
Async XLA Ops:
  57.4 1.5 %copy-start = (f32[9,8,16]{2,1,0:T(8,128)S(1)}, f32[9,8,16]{2,1,0:T(8,128)}, u32[]{:S(2)}) copy-start(f32[9,8,16]{2,1,0:T(8,128)} %get-tuple-element.5) | copy-start | bytes 13828

commit v3 on v2

--- a/solution.py
+++ b/solution.py
@@ -23,7 +23,8 @@
 SOLS = 32
 LANES = 128
 HALF = SOLS // 2
-ROWS = HALF + HALF // 2
+SUB = HALF // 2
+ROWS = 3 * SUB
 FAR = sorted(
     [(dz, dx) for dz in range(SIDE) for dx in range(SIDE) if dz or dx],
     key=lambda d: -sum(min(n, SIDE - n) for n in d),
@@ -54,13 +55,13 @@
     return jnp.where(clear, a, b) + lanes(jnp.where(clear, b, a), lane ^ bit)
 
 
-def merge_all(arrays, lane, top):
+def merge_many(jobs, lane, top):
     bit = top
-    while len(arrays) > 1:
-        half = len(arrays) // 2
-        arrays = [merge(a, b, lane, bit) for a, b in zip(arrays[:half], arrays[half:])]
+    while len(jobs[0]) > 1:
+        half = len(jobs[0]) // 2
+        jobs = [[merge(a, b, lane, bit) for a, b in zip(job[:half], job[half:])] for job in jobs]
         bit //= 2
-    return arrays[0]
+    return [job[0] for job in jobs]
 
 
 def mul(a, b):
@@ -157,8 +158,8 @@
     vis_hbm, mdl_hbm, start_hbm, pen_hbm, pairs_hbm, flags_hbm, chan_hbm,
     gains_out, coeff_out,
     vis, mdl, start, pen_in, pairs, flags, chan, ends,
-    vf, mf, coef, half_out, mine, every, terms, sbuf, rbuf, prec, names, away, wsend, wrec,
-    mixed, final, last, basis, scale, pen, cons, dual, ginv,
+    vf, mf, coef, half_out, mine, every, sbuf, rbuf, prec, names, away, wsend, wrec,
+    hold, jp_at, jq_at, raw, term_g, term_h, named_at, mixed, final, last, basis, scale, pen, cons, dual, ginv,
     loc, ag_s, ag_r, rs_s, rs_r, ps_s, ps_r, one,
 ):
     band = lax.axis_index("band")
@@ -177,6 +178,19 @@
             src_ref=src, dst_ref=dst, send_sem=send, recv_sem=recv,
             device_id=(band_to, base_to), device_id_type=MESH,
         )
+
+    barrier = pltpu.get_barrier_semaphore()
+
+    def greet(band_to, base_to):
+        pl.semaphore_signal(barrier, inc=1, device_id=(band_to, base_to), device_id_type=MESH)
+
+    for dz, dx in FAR:
+        for c in range(2):
+            greet(band, 2 * at(dz, dx) + c)
+    for d in (2, 1, 3):
+        for c in range(2):
+            greet((band + d) % BANDS, 2 * chip + c)
+    greet(band, sibling)
 
     local = [
         pltpu.make_async_copy(src, dst, loc.at[n])
@@ -190,27 +204,12 @@
     for c in local:
         c.start()
 
-    barrier = pltpu.get_barrier_semaphore()
-
-    def greet(band_to, base_to):
-        pl.semaphore_signal(barrier, inc=1, device_id=(band_to, base_to), device_id_type=MESH)
-
-    for dz, dx in FAR:
-        for c in range(2):
-            greet(band, 2 * at(dz, dx) + c)
-    for d in (2, 1, 3):
-        for c in range(2):
-            greet((band + d) % BANDS, 2 * chip + c)
-    greet(band, sibling)
-
     lane8 = iota((8, LANES), 1)
     row8 = iota((8, LANES), 0)
     for c in local[:5]:
         c.wait()
-    mine[...] = start[...].reshape(8 * BLOCK, SOLS).T
-    keep = pl.ds(pl.multiple_of(core * HALF, HALF), HALF)
-    give = pl.ds(pl.multiple_of((1 - core) * HALF, HALF), HALF)
-    every[0, base] = mine[keep, :]
+    mine[...] = start[...].reshape(8 * BLOCK, SOLS).T.reshape(2, 2, SUB, LANES)
+    every[0, base] = mine[core]
 
     for t in range(TILES):
         for side in range(2):
@@ -246,13 +245,17 @@
 
     pl.semaphore_wait(barrier, 2 * CHIPS - 1 + 2 * (BANDS - 1))
 
-    for dz, dx in FAR:
-        for c in range(2):
-            copy(
-                mine.at[pl.ds(HALF * c, HALF)], every.at[0, base], ag_s.at[0], ag_r.at[0],
-                band, 2 * at(dz, dx) + c,
-            ).start()
-    copy(mine.at[give], every.at[0, base], ag_s.at[0], ag_r.at[0], band, sibling).start()
+    def send_start(half, chain, base_to):
+        copy(
+            mine.at[half, chain], every.at[0, base, chain], ag_s.at[chain], ag_r.at[chain],
+            band, base_to,
+        ).start()
+
+    for chain in range(2):
+        for dz, dx in FAR:
+            for c in range(2):
+                send_start(c, chain, 2 * at(dz, dx) + c)
+        send_start(1 - core, chain, sibling)
     names_copy = copy(names.at[0], names.at[1], one.at[0], one.at[1], band, sibling)
     away_copy = copy(away.at[0], away.at[1], one.at[2], one.at[3], band, sibling)
     names_copy.start()
@@ -329,10 +332,14 @@
             wsend.at[k], wrec.at[chip], one.at[6], one.at[7], band, 2 * k + core
         ).start()
     wrec[chip] = weight_rows(chip)
-    own_pen = jnp.broadcast_to(away[0, 4:5, :], (HALF, LANES))
-    its_pen = jnp.broadcast_to(away[1, 4:5, :], (HALF, LANES))
-    pen[0] = jnp.where(core == 0, own_pen, its_pen)
-    pen[1] = jnp.where(core == 0, its_pen, own_pen)
+    own_pen = jnp.broadcast_to(away[0, 4:5, :], (SUB, LANES))
+    its_pen = jnp.broadcast_to(away[1, 4:5, :], (SUB, LANES))
+    pen[...] = jnp.concatenate(
+        [jnp.where(core == 0, own_pen, its_pen), jnp.where(core == 0, its_pen, own_pen)], axis=0
+    )
+    for own in range(2):
+        for e in range(2 * TILES):
+            named_at[2 * TILES * own + e] = jnp.broadcast_to(names[own, e : e + 1, :], (8, LANES))
 
     def arrived(ref, sem):
         pltpu.make_async_copy(ref, ref, sem).wait()
@@ -344,13 +351,16 @@
 
     def along_basis(part):
         return [jnp.sum(basis[k] * part, axis=0, keepdims=True) for k in range(NPOLY)] + pad
+
+    def of_block(b):
+        return jnp.concatenate([mixed[c, SUB * b : SUB * (b + 1), :] for c in range(2)], axis=0)
 
     def total_of(it):
         column = iota((HALF, LANES), 1)
         columns = jnp.zeros((HALF, LANES), F32)
         for k in range(NPOLY):
             columns = jnp.where(column == k, basis[k], columns)
-        out = along_basis(mixed[0]) + along_basis(mixed[1]) + along_basis(columns)
+        out = along_basis(of_block(0)) + along_basis(of_block(1)) + along_basis(columns)
         prec[it, me] = jnp.concatenate(out, axis=0)
 
         def send(band_to, base_to):
@@ -387,15 +397,109 @@
 
         return [solve_gram(total[16 * b : 16 * b + 16, :]) for b in range(2)]
 
+    inner = lane8 % BLOCK
+    station = lane8 // BLOCK
+    natural_g = (lane8 % 8) * BLOCK + (inner // 8) * 8 + station
+    natural_h = (lane8 % 8) * BLOCK + (inner // 8) * 8 + (station % 4) * 2
+    own_blocks = pl.ds(2 * chip, 2)
+
+    def tile_terms(it, c):
+        rows = pl.ds(pl.multiple_of(SUB * c, SUB), SUB)
+        tiles = range(2 * TILES)
+        hold[...] = every[it, :, c]
+        for t in tiles:
+            of_p = hold[ends[t, 0]]
+            of_q = hold[ends[t, 1]]
+            for k in range(8):
+                jq_at[t, k] = lanes(of_q, k * BLOCK + inner)
+                for half in range(2):
+                    jp_at[t, half, k] = lanes(of_p, k * BLOCK + half * 8 + station)
+        for t in tiles:
+            jq = [jq_at[t, k] for k in range(8)]
+            sums = []
+            for half in range(2):
+                jp = [jp_at[t, half, k] for k in range(8)]
+
+                def load(n):
+                    return coef[t, n, rows, pl.ds(half * LANES, LANES)]
+
+                gp, hp, gq, hq = station_terms(load, jp, jq)
+                for n, x in enumerate(gp):
+                    raw[t, 8 * half + n] = x
+                for n, x in enumerate(hp):
+                    raw[t, 16 + 4 * half + n] = x
+                sums.append(gq + hq)
+            for n, (x, y) in enumerate(zip(*sums)):
+                raw[t, 24 + n] = x + y
+        gp = merge_many([[raw[t, n] for n in range(16)] for t in tiles], lane8, 8)
+        gq = merge_many([[raw[t, 24 + n] for n in range(8)] for t in tiles], lane8, 64)
+        hp = merge_many([[raw[t, 16 + n] for n in range(8)] for t in tiles], lane8, 8)
+        hq = merge_many([[raw[t, 32 + n] for n in range(4)] for t in tiles], lane8, 32)
+        hp = [x + lanes(x, lane8 ^ 1) for x in hp]
+        hq = [x + lanes(x, lane8 ^ 64) for x in hq]
+        for t in tiles:
+            term_g[2 * t] = lanes(gp[t], natural_g)
+            term_g[2 * t + 1] = gq[t]
+            term_h[2 * t] = lanes(hp[t], natural_h)
+            term_h[2 * t + 1] = hq[t]
+
+    def share(k):
+        out = [jnp.zeros((SUB, LANES), F32) for _ in range(3)]
+        side = 2 * k + lane8 // 64
+        for e in range(4 * TILES):
+            name = named_at[e]
+            out[0] = out[0] + jnp.where(name == 2 * k, term_g[e], 0.0)
+            out[1] = out[1] + jnp.where(name == 2 * k + 1, term_g[e], 0.0)
+            out[2] = out[2] + jnp.where(name == side, term_h[e], 0.0)
+        return jnp.concatenate(out, axis=0)
+
     lane = iota((HALF, LANES), 1)
-    inner = lane % BLOCK
-
-    def natural(l):
-        return (l % 8) * BLOCK + ((l % BLOCK) // 8) * 8 + l // BLOCK
-
-    own_blocks = pl.ds(2 * chip, 2)
+
+    def solve(it, c):
+        normal = functools.reduce(lambda x, y: x + y, [rbuf[it, c, k] for k in range(CHIPS)])
+        part = lane % BLOCK
+        upper = (lane & BLOCK) != 0
+        sign = jnp.where(upper == (lane < 64), 1.0, -1.0)
+        packed = normal[2 * SUB :, :]
+        outer_part = jnp.concatenate([packed, pltpu.roll(packed, 64, 1)], axis=0)
+        per = scale[c]
+        rho = pen[...]
+        rhs = normal[: 2 * SUB, :] * per + rho * (cons[c] - dual[c])
+        h_diag = lanes(outer_part, jnp.where(upper, part, BLOCK + part)) * per + rho
+        h_real = lanes(outer_part, 2 * BLOCK + part) * per
+        h_imag = lanes(outer_part, 3 * BLOCK + part) * per
+        determ = h_diag * lanes(h_diag, lane ^ BLOCK) - h_real * h_real - h_imag * h_imag
+        return (
+            rhs * h_diag
+            - lanes(rhs, lane ^ BLOCK) * h_real
+            + sign * lanes(rhs, lane ^ (64 + BLOCK)) * h_imag
+        ) / determ
 
     def iteration(it, carry):
+        def send_terms(c, carry):
+            chain = 2 * it + c
+
+            @pl.when(it > 0)
+            def _():
+                arrived(every.at[it, pl.ds(0, 2 * CHIPS - 2), c], ag_r.at[chain])
+
+            @pl.when(it == 0)
+            def _():
+                arrived(every.at[0, pl.ds(0, 2 * CHIPS - 1), c], ag_r.at[c])
+
+            tile_terms(it, c)
+            for dz, dx in FAR:
+                k = at(dz, dx)
+                sbuf[it, c, k] = share(k)
+                copy(
+                    sbuf.at[it, c, k], rbuf.at[it, c, chip], rs_s.at[chain], rs_r.at[chain],
+                    band, 2 * k + core,
+                ).start()
+            rbuf[it, c, chip] = share(chip)
+            return carry
+
+        lax.fori_loop(0, 2, send_terms, 0)
+
         @pl.when(it > 0)
         def _():
             coeff = from_total(total_at(it - 1), it == 1)
@@ -403,111 +507,48 @@
                 agreed = basis[0] * coeff[b][0:1, :]
                 for k in range(1, NPOLY):
                     agreed = agreed + basis[k] * coeff[b][k : k + 1, :]
-                dual[b] = mixed[b] - agreed
-                cons[b] = agreed
-            arrived(every.at[it, pl.ds(0, 2 * CHIPS - 2)], ag_r.at[it])
+                rows = pl.ds(SUB * b, SUB)
+                for c in range(2):
+                    new = agreed[SUB * c : SUB * (c + 1), :]
+                    dual[c, rows] = mixed[c, rows] - new
+                    cons[c, rows] = new
 
         @pl.when(it == 0)
         def _():
-            arrived(every.at[0, pl.ds(0, 2 * CHIPS - 1)], ag_r.at[0])
-            cons[...] = every[0, own_blocks]
+            for c in range(2):
+                for b in range(2):
+                    cons[c, pl.ds(SUB * b, SUB)] = every[0, 2 * chip + b, c]
             dual[...] = jnp.zeros((2, HALF, LANES), F32)
-
-        def tile(t, carry):
-            of_p = every[it, ends[t, 0]]
-            of_q = every[it, ends[t, 1]]
-            jq = [lanes(of_q, k * BLOCK + inner) for k in range(8)]
-            gp, hp, gq, hq = [], [], [], []
-            for half in range(2):
-                jp = [lanes(of_p, k * BLOCK + half * 8 + lane // BLOCK) for k in range(8)]
-
-                def load(n):
-                    return coef[t, n, :, pl.ds(half * LANES, LANES)]
-
-                a, b, c, d = station_terms(load, jp, jq)
-                gp += a
-                hp += b
-                gq.append(c)
-                hq.append(d)
-            terms[2 * t, pl.ds(0, HALF), :] = lanes(merge_all(gp, lane, 8), natural(lane))
-            summed = [x + y for x, y in zip(gq[0], gq[1])]
-            terms[2 * t + 1, pl.ds(0, HALF), :] = merge_all(summed, lane, 64)
-            summed = [x + y for x, y in zip(hq[0], hq[1])]
-            rows = pl.ds(HALF, 8)
-            arrays = [x[:8] for x in hp[:4]] + [x[8:] for x in hp[:4]]
-            arrays += [x[:8] for x in hp[4:]] + [x[8:] for x in hp[4:]]
-            terms[2 * t, rows, :] = lanes(merge_all(arrays, lane8, 8), natural(lane8))
-            arrays = [x[:8] for x in summed] + [x[8:] for x in summed]
-            terms[2 * t + 1, rows, :] = merge_all(arrays, lane8, 64)
-            return carry
-
-        lax.fori_loop(0, 2 * TILES, tile, 0, unroll=2)
-
-        def share(k):
-            out = [jnp.zeros((ROWS, LANES), F32) for _ in range(2)]
-            for own in range(2):
-                for e in range(2 * TILES):
-                    held = terms[2 * TILES * own + e]
-                    for b in range(2):
-                        hit = jnp.where(names[own, e : e + 1, :] == 2 * k + b, 1.0, 0.0)
-                        out[b] = out[b] + hit * held
-            return out
-
-        for dz, dx in FAR:
-            k = at(dz, dx)
-            out = share(k)
-            sbuf[it, k, 0] = out[0]
-            sbuf[it, k, 1] = out[1]
-            copy(
-                sbuf.at[it, k], rbuf.at[it, chip], rs_s.at[it], rs_r.at[it], band, 2 * k + core
-            ).start()
-        out = share(chip)
-        rbuf[it, chip, 0] = out[0]
-        rbuf[it, chip, 1] = out[1]
 
         @pl.when(it == 0)
         def _():
             arrived(wrec.at[pl.ds(0, CHIPS - 1)], one.at[7])
             total = functools.reduce(lambda a, b: a + b, [wrec[k] for k in range(CHIPS)])
-            for b in range(2):
-                at_station = jnp.broadcast_to(total[b : b + 1, :], (HALF, LANES))
-                scale[b] = 1.0 / jnp.maximum(chans[:HALF] * at_station, 1.0)
-
-        arrived(rbuf.at[it, pl.ds(0, CHIPS - 1)], rs_r.at[it])
-
-        part = lane % BLOCK
-        upper = (lane & BLOCK) != 0
-        sign = jnp.where(upper == (lane < 64), 1.0, -1.0)
-        result = []
-        for b in range(2):
-            normal = functools.reduce(lambda x, y: x + y, [rbuf[it, k, b] for k in range(CHIPS)])
-            packed = normal[HALF:, :]
-            outer_part = jnp.concatenate([packed, pltpu.roll(packed, 64, 1)], axis=0)
-            per = scale[b]
-            rho = pen[b]
-            rhs = normal[:HALF, :] * per + rho * (cons[b] - dual[b])
-            h_diag = lanes(outer_part, jnp.where(upper, part, BLOCK + part)) * per + rho
-            h_real = lanes(outer_part, 2 * BLOCK + part) * per
-            h_imag = lanes(outer_part, 3 * BLOCK + part) * per
-            determ = h_diag * lanes(h_diag, lane ^ BLOCK) - h_real * h_real - h_imag * h_imag
-            solved = (
-                rhs * h_diag
-                - lanes(rhs, lane ^ BLOCK) * h_real
-                + sign * lanes(rhs, lane ^ (64 + BLOCK)) * h_imag
-            ) / determ
-            every[it + 1, 2 * chip + b] = solved
-            result.append(solved)
-
-        @pl.when(it + 1 < ITERS)
-        def _():
-            for dz, dx in FAR:
-                copy(
-                    every.at[it + 1, own_blocks], every.at[it + 1, own_blocks],
-                    ag_s.at[it + 1], ag_r.at[it + 1], band, 2 * at(dz, dx) + core,
-                ).start()
-
-        for b in range(2):
-            mixed[b] = result[b] + dual[b]
+            for c in range(2):
+                for b in range(2):
+                    at_station = jnp.broadcast_to(total[b : b + 1, :], (SUB, LANES))
+                    counts = chans[SUB * c : SUB * (c + 1)] * at_station
+                    scale[c, pl.ds(SUB * b, SUB)] = 1.0 / jnp.maximum(counts, 1.0)
+
+        def send_gains(c, carry):
+            chain = 2 * it + c
+            arrived(rbuf.at[it, c, pl.ds(0, CHIPS - 1)], rs_r.at[chain])
+            solved = solve(it, c)
+            every[it + 1, 2 * chip, c] = solved[:SUB]
+            every[it + 1, 2 * chip + 1, c] = solved[SUB:]
+
+            @pl.when(it + 1 < ITERS)
+            def _():
+                for dz, dx in FAR:
+                    copy(
+                        every.at[it + 1, own_blocks, c], every.at[it + 1, own_blocks, c],
+                        ag_s.at[chain + 2], ag_r.at[chain + 2], band, 2 * at(dz, dx) + core,
+                    ).start()
+
+            mixed[c] = solved + dual[c]
+            return carry
+
+        lax.fori_loop(0, 2, send_gains, 0)
 
         @pl.when(it + 1 < ITERS)
         def _():
@@ -518,7 +559,7 @@
     lax.fori_loop(0, ITERS, iteration, 0)
 
     for c in range(2):
-        last[c] = jnp.concatenate(along_basis(mixed[c]), axis=0)
+        last[c] = jnp.concatenate(along_basis(of_block(c)), axis=0)
 
     def send_last(c, band_to, base_to):
         copy(
@@ -536,8 +577,7 @@
     last[2 + me] = last[core]
     final[core] = every[ITERS, base]
     final_copy.wait_recv()
-    gains = jnp.concatenate([final[0], final[1]], axis=0)
-    gains_out[...] = gains.T.reshape(8, BLOCK, SOLS)
+    gains_out[...] = final[...].reshape(SOLS, LANES).T.reshape(8, BLOCK, SOLS)
     arrived(last.at[pl.ds(0, 2 * BANDS - 1)], one.at[11])
     coeff = solve_gram(
         functools.reduce(lambda a, b: a + b, [last[2 + k] for k in range(2 * BANDS)])
@@ -550,11 +590,13 @@
     final_copy.wait_send()
     arrived(half_out, one.at[4])
     arrived(wsend.at[pl.ds(0, CHIPS - 1)], one.at[6])
-    arrived(every.at[0, pl.ds(0, 2 * CHIPS - 1)], ag_s.at[0])
+    for c in range(2):
+        arrived(every.at[0, pl.ds(0, 2 * CHIPS - 1), c], ag_s.at[c])
     for it in range(ITERS):
-        if it > 0:
-            arrived(every.at[it, pl.ds(0, 2 * CHIPS - 2)], ag_s.at[it])
-        arrived(sbuf.at[it, pl.ds(0, CHIPS - 1)], rs_s.at[it])
+        for c in range(2):
+            if it > 0:
+                arrived(every.at[it, pl.ds(0, 2 * CHIPS - 2), c], ag_s.at[2 * it + c])
+            arrived(sbuf.at[it, c, pl.ds(0, CHIPS - 1)], rs_s.at[2 * it + c])
         if it + 1 < ITERS:
             arrived(prec.at[it, pl.ds(0, 2 * BANDS - 1)], ps_s.at[it])
     arrived(last.at[pl.ds(0, 2 * BANDS - 1)], one.at[10])
@@ -583,39 +625,51 @@
             vmem((8, CHANS, CELLS), F32),
             vmem((2 * TILES, NCOEF, HALF, CELLS), F32),
             vmem((TILES, NCOEF, HALF, CELLS), F32),
-            vmem((SOLS, LANES), F32),
-            vmem((ITERS + 1, 2 * CHIPS, HALF, LANES), F32),
-            vmem((4 * TILES, ROWS, LANES), F32),
-            vmem((ITERS, CHIPS, 2, ROWS, LANES), F32),
-            vmem((ITERS, CHIPS, 2, ROWS, LANES), F32),
+            vmem((2, 2, SUB, LANES), F32),
+            vmem((ITERS + 1, 2 * CHIPS, 2, SUB, LANES), F32),
+            vmem((ITERS, 2, CHIPS, ROWS, LANES), F32),
+            vmem((ITERS, 2, CHIPS, ROWS, LANES), F32),
             vmem((ITERS, 2 * BANDS, 48, LANES), F32),
             vmem((2, 8, LANES), jnp.int32),
             vmem((2, 8, LANES), F32),
             vmem((CHIPS, 8, LANES), F32),
             vmem((CHIPS, 8, LANES), F32),
+            vmem((2 * CHIPS, SUB, LANES), F32),
+            vmem((2 * TILES, 2, 8, SUB, LANES), F32),
+            vmem((2 * TILES, 8, SUB, LANES), F32),
+            vmem((2 * TILES, 36, SUB, LANES), F32),
+            vmem((4 * TILES, SUB, LANES), F32),
+            vmem((4 * TILES, SUB, LANES), F32),
+            vmem((4 * TILES, SUB, LANES), jnp.int32),
             vmem((2, HALF, LANES), F32),
-            vmem((2, HALF, LANES), F32),
+            vmem((2, 2, SUB, LANES), F32),
             vmem((2 + 2 * BANDS, 16, LANES), F32),
             vmem((NPOLY, HALF, LANES), F32),
             vmem((2, HALF, LANES), F32),
-            vmem((2, HALF, LANES), F32),
+            vmem((HALF, LANES), F32),
             vmem((2, HALF, LANES), F32),
             vmem((2, HALF, LANES), F32),
             vmem((NPOLY, 16, LANES), F32),
             dma((7,)),
-            *[dma((ITERS,))] * 6,
+            *[dma((2 * ITERS,))] * 4,
+            *[dma((ITERS,))] * 2,
             dma((12,)),
         ],
         compiler_params=pltpu.CompilerParams(
-            collective_id=0, has_side_effects=True, vmem_limit_bytes=60 * 1024 * 1024
+            collective_id=0, has_side_effects=True, vmem_limit_bytes=40 * 1024 * 1024
         ),
         cost_estimate=pl.CostEstimate(
             flops=60_000_000, bytes_accessed=3_000_000, transcendentals=0
         ),
         name="admm",
     )(
-        visibilities, model, jnp.swapaxes(start_gains, 1, 2), penalty.reshape(1, BLOCK), pairs, flags,
-        chan_band.reshape(1, CHANS),
+        *[
+            pltpu.with_memory_space_constraint(x, pltpu.HBM)
+            for x in (
+                visibilities, model, jnp.swapaxes(start_gains, 1, 2), penalty.reshape(1, BLOCK),
+                pairs, flags, chan_band.reshape(1, CHANS),
+            )
+        ]
     )
     return jnp.swapaxes(gains, 1, 2), jnp.swapaxes(coeff, 0, 1)
 

time: 59.7 us -> 52.2 us (0.87)
  Pallas kernels: 56.8 us -> 50.2 us
  local copies, waits for them, and re-layouts: 2.1 us -> 1.25 us
    pallas_call x1, Pallas kernels: 56.8 us -> 50.2 us  [on_device(): pl.pallas_call(kernel, out_shape=(jax.ShapeDtypeStruct((8, BLOCK, SOLS),...]
    unnamed x4 -> x2, local copies, waits for them, and re-layouts: 2.1 us -> 1.25 us
where the time goes in v3:
time: 52.2 us; the launch traced here: 52.1 us
  Pallas kernels  50.2 us (96%)
  local copies, waits for them, and re-layouts  1.25 us (2%)
  between operations  0.64 us (1%)
    pallas_call x1, Pallas kernels, on_device(): pl.pallas_call(kernel, out_shape=(jax.ShapeDtypeStruct((8, BLOCK, SOLS),...  50.2 us
    unnamed x2, local copies, waits for them, and re-layouts  1.25 us

profile of v3, /device:TPU:1, one launch (start us, length us, event | category | flops | bytes accessed | tf_op | source)
XLA Modules:
  0.0 52.1 jit_solution(14021257083064011255)
XLA Ops:
  0.6 50.2 %admm.1 = (f32[8,16,32]{2,1,0:T(8,128)S(1)}, f32[9,8,16]{2,1,0:T(8,128)S(1)}) custom-call(bf16[8,2,64,256]{3,2,1,0:T(8,128)(2,1)} %vis_hbm.1, bf16[8,2,64,256]{3,2,1,0:T(8,128)(2,1)} %mdl_hbm.1, f32[8,16,32]{2,1,0:T(8,128)} %bitcast.7, f32[1,16]{1,0:T(1,128)} %bitcast.8, s32[2,2]{1,0:T(2,128)} %pairs_hbm.1, s32[2,256]{1,0:T(2,128)} %flags_hbm.1, s32[1,64]{1,0:T(1,128)} %bitcast.9), custom_call_target="tpu_custom_call" | custom-call | flops 60000000 | bytes 3000000 | tf_op jit(solution)/shard_map/admm/pallas_call | solution.py:607
  50.8 0.6 %copy.11 = f32[8,32,16]{1,2,0:T(8,128)} copy(f32[8,32,16]{1,2,0:T(8,128)S(1)} %bitcast.5) | data formatting | bytes 32768
  51.5 0.6 %copy.12 = f32[8,9,16]{2,0,1:T(8,128)} copy(f32[8,9,16]{2,0,1:T(8,128)S(1)} %bitcast.6) | data formatting | bytes 9216

commit v4 on v3

--- a/solution.py
+++ b/solution.py
@@ -26,7 +26,7 @@
 SUB = HALF // 2
 ROWS = 3 * SUB
 FAR = sorted(
-    [(dz, dx) for dz in range(SIDE) for dx in range(SIDE) if dz or dx],
+    [(dz, dx) for dx in range(SIDE) for dz in range(SIDE) if dz or dx],
     key=lambda d: -sum(min(n, SIDE - n) for n in d),
 )
 NCOEF = 48
@@ -55,13 +55,9 @@
     return jnp.where(clear, a, b) + lanes(jnp.where(clear, b, a), lane ^ bit)
 
 
-def merge_many(jobs, lane, top):
-    bit = top
-    while len(jobs[0]) > 1:
-        half = len(jobs[0]) // 2
-        jobs = [[merge(a, b, lane, bit) for a, b in zip(job[:half], job[half:])] for job in jobs]
-        bit //= 2
-    return [job[0] for job in jobs]
+def level(jobs, lane, bit):
+    half = len(jobs[0]) // 2
+    return [[merge(a, b, lane, bit) for a, b in zip(job[:half], job[half:])] for job in jobs]
 
 
 def mul(a, b):
@@ -95,37 +91,33 @@
     return q00, q11, q01
 
 
-def station_terms(load, jp, jq):
-    p = [(jp[k], jp[4 + k]) for k in range(4)]
-    q = [(jq[k], jq[4 + k]) for k in range(4)]
+def sum_of(terms):
+    return functools.reduce(lambda a, b: a + b, terms)
+
+
+def station_terms(load, jp, jq, outer_q):
+    p = [(jp[k], jp[4 + k] - jp[k], jp[4 + k] + jp[k]) for k in range(4)]
+    q = [(jq[k], jq[4 + k] - jq[k], jq[4 + k] + jq[k]) for k in range(4)]
     cross = {}
     for ab in range(4):
         for cd in range(4):
-            cross[ab, cd] = (load(4 * ab + cd), load(16 + 4 * ab + cd))
+            n = 4 * ab + cd
+            cross[ab, cd] = (load(n), load(16 + n), load(NCOEF + n))
+    inner = [(b, c) for b in range(2) for c in range(2)]
     gp, gq = [], []
     for a in range(2):
         for d in range(2):
-            gp.append(
-                add(
-                    *[
-                        mul(cross[2 * a + b, 2 * d + c], q[2 * b + c])
-                        for b in range(2)
-                        for c in range(2)
-                    ]
-                )
-            )
-            gq.append(
-                add(
-                    *[
-                        mul_conj(cross[2 * b + a, 2 * c + d], p[2 * b + c])
-                        for b in range(2)
-                        for c in range(2)
-                    ]
-                )
-            )
+            x = [cross[2 * a + b, 2 * d + c] for b, c in inner]
+            both = sum_of(x[n][2] * q[n][0] for n in range(4))
+            re = both - sum_of(x[n][1] * q[n][2] for n in range(4))
+            gp.append((re, both + sum_of(x[n][0] * q[n][1] for n in range(4))))
+            x = [cross[2 * b + a, 2 * c + d] for b, c in inner]
+            both = sum_of(x[n][2] * p[n][0] for n in range(4))
+            re = both + sum_of(x[n][1] * p[n][1] for n in range(4))
+            gq.append((re, sum_of(x[n][0] * p[n][2] for n in range(4)) - both))
     diag = [load(32 + k) for k in range(4)]
     off = {pair: (load(36 + 2 * n), load(37 + 2 * n)) for n, pair in enumerate(PAIRS)}
-    q00, q11, q01 = outer(jq)
+    q00, q11, q01 = outer_q
     two = scaled(q01, 2.0)
     hp = [
         diag[0] * q00 + diag[1] * q11 + mul_conj(conj(off[0, 1]), two)[0],
@@ -305,7 +297,9 @@
         for n, (x, y) in enumerate(PAIRS):
             put(36 + 2 * n, mf[x] * mf[y] + mf[4 + x] * mf[4 + y])
             put(37 + 2 * n, mf[4 + x] * mf[y] - mf[x] * mf[4 + y])
-        copy(half_out.at[t], coef.at[TILES + t], one.at[4], one.at[5], band, sibling).start()
+        copy(
+            half_out.at[t], coef.at[TILES + t, pl.ds(0, NCOEF)], one.at[4], one.at[5], band, sibling
+        ).start()
         return carry
 
     lax.fori_loop(0, TILES, collapse, 0)
@@ -345,6 +339,9 @@
         pltpu.make_async_copy(ref, ref, sem).wait()
 
     arrived(half_out, one.at[5])
+    for t in range(2 * TILES):
+        for n in range(16):
+            coef[t, NCOEF + n] = coef[t, n] + coef[t, 16 + n]
 
     pad = [jnp.zeros((16 - NPOLY, LANES), F32)]
     me = 2 * band + core
@@ -407,23 +404,26 @@
         rows = pl.ds(pl.multiple_of(SUB * c, SUB), SUB)
         tiles = range(2 * TILES)
         hold[...] = every[it, :, c]
-        for t in tiles:
-            of_p = hold[ends[t, 0]]
-            of_q = hold[ends[t, 1]]
-            for k in range(8):
-                jq_at[t, k] = lanes(of_q, k * BLOCK + inner)
-                for half in range(2):
-                    jp_at[t, half, k] = lanes(of_p, k * BLOCK + half * 8 + station)
+        of_p = [hold[ends[t, 0]] for t in tiles]
+        of_q = [hold[ends[t, 1]] for t in tiles]
+        for k in range(8):
+            for t in tiles:
+                jq_at[t, k] = lanes(of_q[t], k * BLOCK + inner)
+        for k in range(8):
+            for half in range(2):
+                for t in tiles:
+                    jp_at[t, half, k] = lanes(of_p[t], k * BLOCK + half * 8 + station)
         for t in tiles:
             jq = [jq_at[t, k] for k in range(8)]
             sums = []
+            outer_q = outer(jq)
             for half in range(2):
                 jp = [jp_at[t, half, k] for k in range(8)]
 
                 def load(n):
                     return coef[t, n, rows, pl.ds(half * LANES, LANES)]
 
-                gp, hp, gq, hq = station_terms(load, jp, jq)
+                gp, hp, gq, hq = station_terms(load, jp, jq, outer_q)
                 for n, x in enumerate(gp):
                     raw[t, 8 * half + n] = x
                 for n, x in enumerate(hp):
@@ -431,12 +431,17 @@
                 sums.append(gq + hq)
             for n, (x, y) in enumerate(zip(*sums)):
                 raw[t, 24 + n] = x + y
-        gp = merge_many([[raw[t, n] for n in range(16)] for t in tiles], lane8, 8)
-        gq = merge_many([[raw[t, 24 + n] for n in range(8)] for t in tiles], lane8, 64)
-        hp = merge_many([[raw[t, 16 + n] for n in range(8)] for t in tiles], lane8, 8)
-        hq = merge_many([[raw[t, 32 + n] for n in range(4)] for t in tiles], lane8, 32)
-        hp = [x + lanes(x, lane8 ^ 1) for x in hp]
-        hq = [x + lanes(x, lane8 ^ 64) for x in hq]
+        gp = [[raw[t, n] for n in range(16)] for t in tiles]
+        hp = [[raw[t, 16 + n] for n in range(8)] for t in tiles]
+        gq = [[raw[t, 24 + n] for n in range(8)] for t in tiles]
+        hq = [[raw[t, 32 + n] for n in range(4)] for t in tiles]
+        gp, hp, gq = level(gp, lane8, 8), level(hp, lane8, 8), level(gq, lane8, 64)
+        gp, hp, gq, hq = [level(x, lane8, b) for x, b in ((gp, 4), (hp, 4), (gq, 32), (hq, 32))]
+        gp, hp, gq, hq = [level(x, lane8, b) for x, b in ((gp, 2), (hp, 2), (gq, 16), (hq, 16))]
+        gp = [x for (x,) in level(gp, lane8, 1)]
+        hp = [x + lanes(x, lane8 ^ 1) for (x,) in hp]
+        gq = [x for (x,) in gq]
+        hq = [x + pltpu.roll(x, 64, 1) for (x,) in hq]
         for t in tiles:
             term_g[2 * t] = lanes(gp[t], natural_g)
             term_g[2 * t + 1] = gq[t]
@@ -461,14 +466,16 @@
         upper = (lane & BLOCK) != 0
         sign = jnp.where(upper == (lane < 64), 1.0, -1.0)
         packed = normal[2 * SUB :, :]
-        outer_part = jnp.concatenate([packed, pltpu.roll(packed, 64, 1)], axis=0)
+        both = jnp.concatenate([packed, packed], axis=0)
+        part = part + 64 * (iota((HALF, LANES), 0) // SUB)
         per = scale[c]
         rho = pen[...]
         rhs = normal[: 2 * SUB, :] * per + rho * (cons[c] - dual[c])
-        h_diag = lanes(outer_part, jnp.where(upper, part, BLOCK + part)) * per + rho
-        h_real = lanes(outer_part, 2 * BLOCK + part) * per
-        h_imag = lanes(outer_part, 3 * BLOCK + part) * per
-        determ = h_diag * lanes(h_diag, lane ^ BLOCK) - h_real * h_real - h_imag * h_imag
+        h_diag = lanes(both, jnp.where(upper, part, BLOCK + part)) * per + rho
+        h_swap = lanes(both, jnp.where(upper, BLOCK + part, part)) * per + rho
+        h_real = lanes(both, 2 * BLOCK + part) * per
+        h_imag = lanes(both, 3 * BLOCK + part) * per
+        determ = h_diag * h_swap - h_real * h_real - h_imag * h_imag
         return (
             rhs * h_diag
             - lanes(rhs, lane ^ BLOCK) * h_real
@@ -623,7 +630,7 @@
             pltpu.SMEM((2 * TILES, 2), jnp.int32),
             vmem((8, CHANS, CELLS), F32),
             vmem((8, CHANS, CELLS), F32),
-            vmem((2 * TILES, NCOEF, HALF, CELLS), F32),
+            vmem((2 * TILES, NCOEF + 16, HALF, CELLS), F32),
             vmem((TILES, NCOEF, HALF, CELLS), F32),
             vmem((2, 2, SUB, LANES), F32),
             vmem((ITERS + 1, 2 * CHIPS, 2, SUB, LANES), F32),

time: 52.2 us -> 51.3 us (0.983)
  Pallas kernels: 50.2 us -> 49.3 us
    pallas_call x1, Pallas kernels: 50.2 us -> 49.3 us  [on_device(): pl.pallas_call(kernel, out_shape=(jax.ShapeDtypeStruct((8, BLOCK, SOLS),...]
where the time goes in v4:
time: 51.3 us; the launch traced here: 51.2 us
  Pallas kernels  49.3 us (96%)
  local copies, waits for them, and re-layouts  1.25 us (2%)
  between operations  0.64 us (1%)
    pallas_call x1, Pallas kernels, on_device(): pl.pallas_call(kernel, out_shape=(jax.ShapeDtypeStruct((8, BLOCK, SOLS),...  49.3 us
    unnamed x2, local copies, waits for them, and re-layouts  1.25 us

profile of v4, /device:TPU:1, one launch (start us, length us, event | category | flops | bytes accessed | tf_op | source)
XLA Modules:
  0.0 51.2 jit_solution(7697910149494827814)
XLA Ops:
  0.6 49.3 %admm.1 = (f32[8,16,32]{2,1,0:T(8,128)S(1)}, f32[9,8,16]{2,1,0:T(8,128)S(1)}) custom-call(bf16[8,2,64,256]{3,2,1,0:T(8,128)(2,1)} %vis_hbm.1, bf16[8,2,64,256]{3,2,1,0:T(8,128)(2,1)} %mdl_hbm.1, f32[8,16,32]{2,1,0:T(8,128)} %bitcast.7, f32[1,16]{1,0:T(1,128)} %bitcast.8, s32[2,2]{1,0:T(2,128)} %pairs_hbm.1, s32[2,256]{1,0:T(2,128)} %flags_hbm.1, s32[1,64]{1,0:T(1,128)} %bitcast.9), custom_call_target="tpu_custom_call" | custom-call | flops 60000000 | bytes 3000000 | tf_op jit(solution)/shard_map/admm/pallas_call | solution.py:614
  49.9 0.6 %copy.11 = f32[8,32,16]{1,2,0:T(8,128)} copy(f32[8,32,16]{1,2,0:T(8,128)S(1)} %bitcast.5) | data formatting | bytes 32768
  50.6 0.6 %copy.12 = f32[8,9,16]{2,0,1:T(8,128)} copy(f32[8,9,16]{2,0,1:T(8,128)S(1)} %bitcast.6) | data formatting | bytes 9216

commit v5 on v4

--- a/solution.py
+++ b/solution.py
@@ -266,7 +266,7 @@
         cheb.append(2.0 * centre * cheb[-1] - cheb[-2])
     for k in range(NPOLY):
         basis[k] = cheb[k]
-    member2 = jnp.concatenate([member, member], axis=1).astype(BF16)
+    member3 = jnp.concatenate([member] * 3, axis=1).astype(BF16)
 
     for c in local[5:]:
         c.wait()
@@ -279,9 +279,11 @@
 
         def put(n, product):
             high = product.astype(BF16)
-            low = (product - high.astype(F32)).astype(BF16)
+            rest = product - high.astype(F32)
+            middle = rest.astype(BF16)
+            low = (rest - middle.astype(F32)).astype(BF16)
             out = jnp.dot(
-                member2, jnp.concatenate([high, low], axis=0), preferred_element_type=F32
+                member3, jnp.concatenate([high, middle, low], axis=0), preferred_element_type=F32
             )
             coef[t, n] = out[:HALF]
             half_out[t, n] = out[HALF:]

time: 51.3 us -> 50.9 us (level)
  no operation moved by 1% of the time
where the time goes in v5:
time: 50.9 us; the launch traced here: 50.8 us
  Pallas kernels  48.9 us (96%)
  local copies, waits for them, and re-layouts  1.25 us (2%)
  between operations  0.64 us (1%)
    pallas_call x1, Pallas kernels, on_device(): pl.pallas_call(kernel, out_shape=(jax.ShapeDtypeStruct((8, BLOCK, SOLS),...  48.9 us
    unnamed x2, local copies, waits for them, and re-layouts  1.25 us

profile of v5, /device:TPU:1, one launch (start us, length us, event | category | flops | bytes accessed | tf_op | source)
XLA Modules:
  0.0 50.8 jit_solution(886853347193529853)
XLA Ops:
  0.6 48.9 %admm.1 = (f32[8,16,32]{2,1,0:T(8,128)S(1)}, f32[9,8,16]{2,1,0:T(8,128)S(1)}) custom-call(bf16[8,2,64,256]{3,2,1,0:T(8,128)(2,1)} %vis_hbm.1, bf16[8,2,64,256]{3,2,1,0:T(8,128)(2,1)} %mdl_hbm.1, f32[8,16,32]{2,1,0:T(8,128)} %bitcast.7, f32[1,16]{1,0:T(1,128)} %bitcast.8, s32[2,2]{1,0:T(2,128)} %pairs_hbm.1, s32[2,256]{1,0:T(2,128)} %flags_hbm.1, s32[1,64]{1,0:T(1,128)} %bitcast.9), custom_call_target="tpu_custom_call" | custom-call | flops 60000000 | bytes 3000000 | tf_op jit(solution)/shard_map/admm/pallas_call | solution.py:616
  49.6 0.6 %copy.11 = f32[8,32,16]{1,2,0:T(8,128)} copy(f32[8,32,16]{1,2,0:T(8,128)S(1)} %bitcast.5) | data formatting | bytes 32768
  50.2 0.6 %copy.12 = f32[8,9,16]{2,0,1:T(8,128)} copy(f32[8,9,16]{2,0,1:T(8,128)S(1)} %bitcast.6) | data formatting | bytes 9216

commit v6 on v5

--- a/solution.py
+++ b/solution.py
@@ -507,7 +507,7 @@
             rbuf[it, c, chip] = share(chip)
             return carry
 
-        lax.fori_loop(0, 2, send_terms, 0)
+        lax.fori_loop(0, 2, send_terms, 0, unroll=True)
 
         @pl.when(it > 0)
         def _():
@@ -557,7 +557,7 @@
             mixed[c] = solved + dual[c]
             return carry
 
-        lax.fori_loop(0, 2, send_gains, 0)
+        lax.fori_loop(0, 2, send_gains, 0, unroll=True)
 
         @pl.when(it + 1 < ITERS)
         def _():

time: 50.9 us -> 51 us (level)
  no operation moved by 1% of the time
where the time goes in v6:
time: 51 us; the launch traced here: 50.8 us
  Pallas kernels  48.9 us (96%)
  local copies, waits for them, and re-layouts  1.25 us (2%)
  between operations  0.64 us (1%)
    pallas_call x1, Pallas kernels, on_device(): pl.pallas_call(kernel, out_shape=(jax.ShapeDtypeStruct((8, BLOCK, SOLS),...  48.9 us
    unnamed x2, local copies, waits for them, and re-layouts  1.25 us

profile of v6, /device:TPU:1, one launch (start us, length us, event | category | flops | bytes accessed | tf_op | source)
XLA Modules:
  0.0 50.8 jit_solution(17909193779294133713)
XLA Ops:
  0.6 48.9 %admm.1 = (f32[8,16,32]{2,1,0:T(8,128)S(1)}, f32[9,8,16]{2,1,0:T(8,128)S(1)}) custom-call(bf16[8,2,64,256]{3,2,1,0:T(8,128)(2,1)} %vis_hbm.1, bf16[8,2,64,256]{3,2,1,0:T(8,128)(2,1)} %mdl_hbm.1, f32[8,16,32]{2,1,0:T(8,128)} %bitcast.7, f32[1,16]{1,0:T(1,128)} %bitcast.8, s32[2,2]{1,0:T(2,128)} %pairs_hbm.1, s32[2,256]{1,0:T(2,128)} %flags_hbm.1, s32[1,64]{1,0:T(1,128)} %bitcast.9), custom_call_target="tpu_custom_call" | custom-call | flops 60000000 | bytes 3000000 | tf_op jit(solution)/shard_map/admm/pallas_call | solution.py:616
  49.6 0.6 %copy.11 = f32[8,32,16]{1,2,0:T(8,128)} copy(f32[8,32,16]{1,2,0:T(8,128)S(1)} %bitcast.5) | data formatting | bytes 32768
  50.2 0.6 %copy.12 = f32[8,9,16]{2,0,1:T(8,128)} copy(f32[8,9,16]{2,0,1:T(8,128)S(1)} %bitcast.6) | data formatting | bytes 9216
